TPU v7x, 32 devices: a whole 2x2x4 slice. The times are simulated.
32 devices in a mesh: dp: 8 (over z, y), expert: 4 (over x, core).
Axes of the slice: x: 2, y: 2, z: 4, core: 2. Of those that a mesh axis runs over, the one named last changes fastest.
Arguments:
- tokens: bfloat16 [50176, 384], P(('dp', 'expert')), may hold values from -6 to 6
- ln1_gain: float32 [384], replicated, may hold values from 0.5 to 1.5
- ln1_bias: float32 [384], replicated, may hold values from -1.75 to 1.75
- qkv_weight: bfloat16 [384, 1152], replicated, may hold values from -0.3125 to 0.3125
- q_bias: float32 [384], replicated, may hold values from -1.75 to 1.75
- v_bias: float32 [384], replicated, may hold values from -1.75 to 1.75
- bias_table: float32 [169, 12], replicated, may hold values from -6 to 6
- out_weight: bfloat16 [384, 384], replicated, may hold values from -0.625 to 0.625
- out_bias: float32 [384], replicated, may hold values from -1.75 to 1.75
- ln2_gain: float32 [384], replicated, may hold values from 0.5 to 1.5
- ln2_bias: float32 [384], replicated, may hold values from -1.75 to 1.75
- router_weight: float32 [384, 8], replicated, may hold values from -0.21875 to 0.21875
- up_weight: bfloat16 [8, 384, 1536], P('expert'), may hold values from -0.3125 to 0.3125
- up_bias: float32 [8, 1536], P('expert'), may hold values from -0.625 to 0.625
- down_weight: bfloat16 [8, 1536, 384], P('expert'), may hold values from -1.25 to 1.25
- down_bias: float32 [8, 384], P('expert'), may hold values from -2.5 to 2.5
- expert_of: int32 [50176], P(('dp', 'expert')), may hold values from 0 to 7, as said below
- slot_of: int32 [50176], P(('dp', 'expert')), may hold values from -1 to 244, as said below
- grad_output: bfloat16 [50176, 384], P(('dp', 'expert')), may hold values from -6 to 6
Outputs:
- output: bfloat16 [50176, 384], P(('dp', 'expert'))
- grad_tokens: float32 [50176, 384], P(('dp', 'expert'))
- grad_ln1_gain: float32 [384], replicated
- grad_ln1_bias: float32 [384], replicated
- grad_qkv_weight: float32 [384, 1152], replicated
- grad_q_bias: float32 [384], replicated
- grad_v_bias: float32 [384], replicated
- grad_bias_table: float32 [169, 12], replicated
- grad_out_weight: float32 [384, 384], replicated
- grad_out_bias: float32 [384], replicated
- grad_ln2_gain: float32 [384], replicated
- grad_ln2_bias: float32 [384], replicated
- grad_router_weight: float32 [384, 8], replicated
- grad_up_weight: float32 [8, 384, 1536], P('expert')
- grad_up_bias: float32 [8, 1536], P('expert')
- grad_down_weight: float32 [8, 1536, 384], P('expert')
- grad_down_bias: float32 [8, 384], P('expert')
Inputs may be any that keep to these rules, and one draw needn't show every extreme that they name: `expert_of`: in every aligned block of 1568 tokens (one device's) some expert is named by more than 245 tokens. `slot_of`: the token's rank in token order among the tokens of its block of 1568 with the same expert, where that rank is below 245; -1 otherwise.
All inputs are finite; a program needn't handle non-finite values.
Results may differ from a plain program's by a relative error of at most 0.015.
Values may be sent and summed in bfloat16 or wider, within the bound.
A program may use at most 192 MiB of HBM per device.

v0:
```python
from functools import partial

import jax
import jax.numpy as jnp
from jax import lax
from jax.sharding import PartitionSpec as P

D = 384
HEADS = 12
HEAD = 32
EXPERTS = 8
WINDOW = 7
SIDE = 14
SHIFT = 3
CAP = 245


EPSILON = 1e-05
MASK_NEG = -100.0
HIGHEST = lax.Precision.HIGHEST


def layer_norm(inputs, scaling, offset):
    center = inputs - jnp.mean(inputs, axis=-1, keepdims=True)
    spread = jnp.mean(center * center, axis=-1, keepdims=True)
    return center * lax.rsqrt(spread + EPSILON) * scaling + offset


def to_windows(grid):
    image_count = grid.shape[0]
    channels = grid.shape[-1]
    per_side = SIDE // WINDOW
    split = grid.reshape(image_count, per_side, WINDOW, per_side, WINDOW, channels)
    return split.transpose(0, 1, 3, 2, 4, 5).reshape(
        image_count * per_side * per_side, WINDOW * WINDOW, channels
    )


def from_windows(windows, image_count):
    channels = windows.shape[-1]
    per_side = SIDE // WINDOW
    split = windows.reshape(image_count, per_side, per_side, WINDOW, WINDOW, channels)
    return split.transpose(0, 1, 3, 2, 4, 5).reshape(image_count, SIDE, SIDE, channels)


def shift_in(rows_in, image_count):
    grid = rows_in.reshape(image_count, SIDE, SIDE, rows_in.shape[-1])
    return to_windows(jnp.roll(grid, (-SHIFT, -SHIFT), axis=(1, 2)))


def shift_out(windows, image_count):
    grid = jnp.roll(from_windows(windows, image_count), (SHIFT, SHIFT), axis=(1, 2))
    return grid.reshape(image_count * SIDE * SIDE, windows.shape[-1])


def window_mask(image_count):
    places = jnp.arange(SIDE)
    bands = (places >= SIDE - WINDOW).astype(jnp.int32) + (places >= SIDE - SHIFT).astype(jnp.int32)
    regions = (bands[:, None] * 3 + bands[None, :]).reshape(1, SIDE, SIDE, 1)
    labels = to_windows(regions)[:, :, 0]
    masked = jnp.where(labels[:, :, None] != labels[:, None, :], MASK_NEG, 0.0).astype(jnp.float32)
    return jnp.tile(masked, (image_count, 1, 1))


def position_table():
    cells = jnp.arange(WINDOW * WINDOW)
    rowpos = cells // WINDOW
    colpos = cells % WINDOW
    index_map = (rowpos[:, None] - rowpos[None, :] + WINDOW - 1) * (2 * WINDOW - 1) + (
        colpos[:, None] - colpos[None, :] + WINDOW - 1
    )
    return (index_map[:, :, None] == jnp.arange((2 * WINDOW - 1) ** 2)).astype(jnp.float32)


def router_gates(normed_float, router_weight, chosen):
    router_probs = jax.nn.softmax(jnp.dot(normed_float, router_weight, precision=HIGHEST), axis=-1)
    return jnp.sum(router_probs * chosen, axis=-1)


def exact_gelu(inputs):
    return jax.nn.gelu(inputs, approximate=False)


def matmul(left, right):
    return jnp.dot(left, right, preferred_element_type=jnp.float32)


def matmul_tn(left, right):
    return lax.dot_general(
        left, right, (((0,), (0,)), ((), ())), preferred_element_type=jnp.float32
    )


def matmul_nt(left, right):
    return lax.dot_general(
        left, right, (((1,), (1,)), ((), ())), preferred_element_type=jnp.float32
    )


def shards(
    tokens,
    ln1_gain,
    ln1_bias,
    qkv_weight,
    q_bias,
    v_bias,
    bias_table,
    out_weight,
    out_bias,
    ln2_gain,
    ln2_bias,
    router_weight,
    up_weight,
    up_bias,
    down_weight,
    down_bias,
    expert_of,
    slot_of,
    grad_output,
):
    members = lax.axis_size("expert")
    local_count = up_weight.shape[0]
    row_count = tokens.shape[0]
    image_count = row_count // (SIDE * SIDE)
    window_cells = WINDOW * WINDOW
    score_scale = HEAD ** (-0.5)
    inputs = tokens.astype(jnp.float32)
    normed, norm_one_pull = jax.vjp(layer_norm, inputs, ln1_gain, ln1_bias)
    normed_low = normed.astype(jnp.bfloat16)
    qkv_offset = jnp.concatenate([q_bias, jnp.zeros_like(q_bias), v_bias])
    projected = (matmul(normed_low, qkv_weight) + qkv_offset).astype(jnp.bfloat16)
    windows = shift_in(projected, image_count).reshape(-1, window_cells, 3, HEADS, HEAD)
    queries, keys_win, values_win = (windows[:, :, 0], windows[:, :, 1], windows[:, :, 2])
    table_onehot = position_table()
    relative = jnp.einsum("pqt,th->hpq", table_onehot, bias_table, precision=HIGHEST)
    additive = relative[None] + window_mask(image_count)[:, None]

    def score_block(queries_in, keys_in):
        raw_scores = jnp.einsum(
            "wphd,wqhd->whpq", queries_in, keys_in, preferred_element_type=jnp.float32
        )
        return raw_scores * score_scale + additive

    scores = score_block(queries, keys_win)
    log_total = jax.nn.logsumexp(scores, axis=-1, keepdims=True)
    weights_low = jnp.exp(scores - log_total).astype(jnp.bfloat16)
    attended = jnp.einsum(
        "whpq,wqhd->wphd", weights_low, values_win, preferred_element_type=jnp.float32
    )
    attended_low = shift_out(
        attended.reshape(-1, window_cells, D).astype(jnp.bfloat16), image_count
    )
    residual = inputs + matmul(attended_low, out_weight) + out_bias
    normed_two, norm_two_pull = jax.vjp(layer_norm, residual, ln2_gain, ln2_bias)
    normed_two_low = normed_two.astype(jnp.bfloat16)
    chosen = (expert_of[:, None] == jnp.arange(EXPERTS)).astype(jnp.float32)
    gate_values, gate_pull = jax.vjp(
        partial(router_gates, chosen=chosen), normed_two_low.astype(jnp.float32), router_weight
    )
    places = expert_of * CAP + slot_of
    dispatch = ((places[:, None] == jnp.arange(EXPERTS * CAP)) & (slot_of[:, None] >= 0)).astype(
        jnp.bfloat16
    )
    outgoing = (
        matmul_tn(dispatch, normed_two_low)
        .astype(jnp.bfloat16)
        .reshape(members, local_count, CAP, D)
    )
    upstream = grad_output.astype(jnp.float32)
    weighted_low = (gate_values[:, None] * upstream).astype(jnp.bfloat16)
    grad_send = (
        matmul_tn(dispatch, weighted_low).astype(jnp.bfloat16).reshape(members, local_count, CAP, D)
    )
    arrived = lax.all_to_all(outgoing, "expert", split_axis=0, concat_axis=0, tiled=True)
    expert_rows = arrived.transpose(1, 0, 2, 3).reshape(local_count, members * CAP, D)
    hidden_pre = (
        jnp.einsum("erd,edf->erf", expert_rows, up_weight, preferred_element_type=jnp.float32)
        + up_bias[:, None]
    )
    hidden_low = exact_gelu(hidden_pre).astype(jnp.bfloat16)
    expert_out = (
        jnp.einsum("erf,efd->erd", hidden_low, down_weight, preferred_element_type=jnp.float32)
        + down_bias[:, None]
    )
    sending = (
        expert_out.astype(jnp.bfloat16).reshape(local_count, members, CAP, D).transpose(1, 0, 2, 3)
    )
    expert_rows, hidden_pre, hidden_low, sending = (expert_rows, hidden_pre, hidden_low, sending)
    returned = lax.all_to_all(sending, "expert", split_axis=0, concat_axis=0, tiled=True).reshape(
        EXPERTS * CAP, D
    )
    grad_arrived = lax.all_to_all(grad_send, "expert", split_axis=0, concat_axis=0, tiled=True)
    grad_expert_out = grad_arrived.transpose(1, 0, 2, 3).reshape(local_count, members * CAP, D)
    grad_down = jnp.einsum(
        "erf,erd->efd", hidden_low, grad_expert_out, preferred_element_type=jnp.float32
    )
    grad_down_bias = jnp.sum(grad_expert_out.astype(jnp.float32), axis=1)
    grad_hidden = jnp.einsum(
        "erd,efd->erf", grad_expert_out, down_weight, preferred_element_type=jnp.float32
    )
    gelu_value, gelu_pull = jax.vjp(exact_gelu, hidden_pre)
    grad_pre_low = gelu_pull(grad_hidden)[0].astype(jnp.bfloat16)
    grad_up = jnp.einsum(
        "erd,erf->edf", expert_rows, grad_pre_low, preferred_element_type=jnp.float32
    )
    grad_up_bias = jnp.sum(grad_pre_low.astype(jnp.float32), axis=1)
    grad_rows = jnp.einsum(
        "erf,edf->erd", grad_pre_low, up_weight, preferred_element_type=jnp.float32
    ).astype(jnp.bfloat16)
    grad_rows_out = grad_rows.reshape(local_count, members, CAP, D).transpose(1, 0, 2, 3)
    grad_up, grad_up_bias, grad_down, grad_down_bias, grad_rows_out = (
        grad_up,
        grad_up_bias,
        grad_down,
        grad_down_bias,
        grad_rows_out,
    )
    grad_back = lax.all_to_all(
        grad_rows_out, "expert", split_axis=0, concat_axis=0, tiled=True
    ).reshape(EXPERTS * CAP, D)
    combined = matmul(dispatch, returned)
    output = (residual + gate_values[:, None] * combined).astype(jnp.bfloat16)
    gate_grad = jnp.sum(upstream * combined, axis=-1)
    grad_normed_two = matmul(dispatch, grad_back)
    router_input_grad, grad_router = gate_pull(gate_grad)
    grad_resid_norm, grad_ln2_gain, grad_ln2_bias = norm_two_pull(
        grad_normed_two + router_input_grad
    )
    grad_residual = upstream + grad_resid_norm
    grad_mixed_low = grad_residual.astype(jnp.bfloat16)
    grad_out_weight = matmul_tn(attended_low, grad_mixed_low)
    grad_out_bias = jnp.sum(grad_mixed_low.astype(jnp.float32), axis=0)
    grad_attended = matmul_nt(grad_mixed_low, out_weight).astype(jnp.bfloat16)
    grad_windows = shift_in(grad_attended, image_count).reshape(-1, window_cells, HEADS, HEAD)
    weights_back = jnp.exp(score_block(queries, keys_win) - log_total)
    grad_weights = jnp.einsum(
        "wphd,wqhd->whpq", grad_windows, values_win, preferred_element_type=jnp.float32
    )
    grad_values = jnp.einsum(
        "whpq,wphd->wqhd",
        weights_back.astype(jnp.bfloat16),
        grad_windows,
        preferred_element_type=jnp.float32,
    )
    grad_scores = weights_back * (
        grad_weights - jnp.sum(weights_back * grad_weights, axis=-1, keepdims=True)
    )
    grad_scores_low = grad_scores.astype(jnp.bfloat16)
    score_totals = jnp.sum(grad_scores_low.astype(jnp.float32), axis=0)
    grad_table = jnp.einsum("pqt,hpq->th", table_onehot, score_totals, precision=HIGHEST)
    grad_queries = (
        jnp.einsum("whpq,wqhd->wphd", grad_scores_low, keys_win, preferred_element_type=jnp.float32)
        * score_scale
    )
    grad_keys = (
        jnp.einsum("whpq,wphd->wqhd", grad_scores_low, queries, preferred_element_type=jnp.float32)
        * score_scale
    )
    stacked = jnp.stack([grad_queries, grad_keys, grad_values], axis=2).reshape(
        -1, window_cells, 3 * D
    )
    grad_projected = shift_out(stacked.astype(jnp.bfloat16), image_count)
    grad_qkv_weight = matmul_tn(normed_low, grad_projected)
    grad_qkv_offset = jnp.sum(grad_projected.astype(jnp.float32), axis=0)
    grad_q_bias = grad_qkv_offset[:D]
    grad_v_bias = grad_qkv_offset[2 * D :]
    grad_normed = matmul_nt(grad_projected, qkv_weight)
    grad_input_norm, grad_ln1_gain, grad_ln1_bias = norm_one_pull(grad_normed)
    grad_tokens = grad_residual + grad_input_norm
    (
        grad_ln1_gain,
        grad_ln1_bias,
        grad_qkv_weight,
        grad_q_bias,
        grad_v_bias,
        grad_table,
        grad_out_weight,
        grad_out_bias,
        grad_ln2_gain,
        grad_ln2_bias,
        grad_router,
    ) = lax.psum(
        (
            grad_ln1_gain,
            grad_ln1_bias,
            grad_qkv_weight,
            grad_q_bias,
            grad_v_bias,
            grad_table,
            grad_out_weight,
            grad_out_bias,
            grad_ln2_gain,
            grad_ln2_bias,
            grad_router,
        ),
        ("dp", "expert"),
    )
    grad_up, grad_up_bias, grad_down, grad_down_bias = (
        lax.psum(grad_up.astype(jnp.bfloat16), "dp").astype(jnp.float32),
        lax.psum(grad_up_bias.astype(jnp.bfloat16), "dp").astype(jnp.float32),
        lax.psum(grad_down.astype(jnp.bfloat16), "dp").astype(jnp.float32),
        lax.psum(grad_down_bias.astype(jnp.bfloat16), "dp").astype(jnp.float32),
    )
    return (
        output,
        grad_tokens,
        grad_ln1_gain,
        grad_ln1_bias,
        grad_qkv_weight,
        grad_q_bias,
        grad_v_bias,
        grad_table,
        grad_out_weight,
        grad_out_bias,
        grad_ln2_gain,
        grad_ln2_bias,
        grad_router,
        grad_up,
        grad_up_bias,
        grad_down,
        grad_down_bias,
    )


def solution(mesh):
    return jax.shard_map(
        shards,
        mesh=mesh,
        in_specs=(
            P(("dp", "expert"), None),
            P(),
            P(),
            P(),
            P(),
            P(),
            P(),
            P(),
            P(),
            P(),
            P(),
            P(),
            P("expert", None, None),
            P("expert", None),
            P("expert", None, None),
            P("expert", None),
            P(("dp", "expert")),
            P(("dp", "expert")),
            P(("dp", "expert"), None),
        ),
        out_specs=(
            P(("dp", "expert"), None),
            P(("dp", "expert"), None),
            P(),
            P(),
            P(),
            P(),
            P(),
            P(),
            P(),
            P(),
            P(),
            P(),
            P(),
            P("expert", None, None),
            P("expert", None),
            P("expert", None, None),
            P("expert", None),
        ),
        check_vma=False,
    )
```

profile of v0, /device:TPU:0, one launch (start us, length us, event | category | flops | bytes accessed | tf_op | source)
XLA Modules:
  0.0 708.0 jit_solution(17629748459180214983)
XLA Ops:
  12.2 5.7 fusion.16
  17.9 6.6 reshape.337
  25.8 3.9 slice.100
  40.8 4.6 copy.69
  45.4 23.3 %reshape_reshape.7 = bf16[32,49,3,12,32]{4,3,2,0,1:T(8,128)(2,1)} reshape(bf16[8,2,2,7,7,1152]{5,2,1,0,4,3:T(2,128)(2,1)} %copy.69) | data formatting | bytes 7225344 | tf_op jit(solution)/shard_map/reshape;reshape | solution.py:132
  68.7 16.1 %fusion.106 = (bf16[32,49,1,12,32]{4,3,2,0,1:T(8,128)(2,1)}, bf16[32,49,1,12,32]{4,3,2,0,1:T(8,128)(2,1)}, bf16[32,49,1,12,32]{4,3,2,0,1:T(8,128)(2,1)}) fusion(bf16[32,49,3,12,32]{4,3,2,0,1:T(8,128)(2,1)} %reshape_reshape.7), kind=kLoop, calls=%fused_computation.172 | loop fusion | bytes 7225344 | tf_op jit(solution)/shard_map/slice | solution.py:133
  84.9 8.5 %copy.104 = bf16[32,49,1,12,32]{1,4,3,0,2:T(8,128)(2,1)} copy(bf16[32,49,1,12,32]{4,3,2,0,1:T(8,128)(2,1)} %get-tuple-element.53) | data formatting | bytes 2408448
  93.4 8.5 %copy.103 = bf16[32,49,1,12,32]{1,4,3,0,2:T(8,128)(2,1)} copy(bf16[32,49,1,12,32]{4,3,2,0,1:T(8,128)(2,1)} %get-tuple-element.54) | data formatting | bytes 2408448
  101.9 8.7 %copy.105 = bf16[32,49,1,12,32]{1,4,3,0,2:T(8,128)(2,1)} copy(bf16[32,49,1,12,32]{4,3,2,0,1:T(8,128)(2,1)} %get-tuple-element.55) | data formatting | bytes 2408448
  110.7 6.2 fusion.108
  124.8 9.0 %copy.75 = bf16[32,49,12,32]{3,2,0,1:T(8,128)(2,1)} copy(bf16[32,49,12,32]{1,3,2,0:T(8,128)(2,1)} %convert_bitcast_fusion.1) | data formatting | bytes 2408448 | tf_op jit(solution)/shard_map/convert_element_type | solution.py:151
  133.8 9.1 %convert_element_type.133 = bf16[8,2,2,7,7,384]{5,2,1,0,4,3:T(2,128)(2,1)} reshape(bf16[32,49,12,32]{3,2,0,1:T(8,128)(2,1)} %copy.75) | data formatting | bytes 2408448 | tf_op jit(solution)/shard_map/convert_element_type | solution.py:151
  155.2 5.7 fusion.48
  166.4 23.5 %all_to_all.20 = bf16[4,2,245,384]{3,1,2,0:T(2,128)(2,1)S(1)} all-to-all(bf16[4,2,245,384]{3,1,2,0:T(2,128)(2,1)S(1)} %copy.78), channel_id=1, replica_groups=mesh['dp'=8,'expert'=4] {'expert'}, dimensions={0} | all-to-all | bytes 3010560 | tf_op jit(solution)/shard_map/all_to_all | solution.py:174
  190.0 10.0 %fusion.45 = (u8[980,1536]{1,0:T(8,128)(4,1)S(1)}, u8[980,1536]{1,0:T(8,128)(4,1)S(1)}, f32[2,980,1536]{2,1,0:T(8,128)}) fusion(f32[2,1536]{1,0:T(2,128)S(1)} %copy-done.41, bf16[2,384,1536]{2,1,0:T(8,128)(2,1)S(1)} %copy-done, bf16[2,980,384]{2,0,1:T(2,128)(2,1)S(1)} %bitcast.121), kind=kOutput, calls=%fused_computation.86 | convolution fusion | flops 2351247360 | bytes 18929664 | tf_op jit(solution)/shard_map/erd,edf->erf/dot_general | solution.py:177
  200.0 30.8 %multiply_convert_fusion = (bf16[2,980,1536]{2,1,0:T(8,128)(2,1)S(1)}, f32[2,980,1536]{2,1,0:T(8,128)}) fusion(f32[2,980,1536]{2,1,0:T(8,128)} %get-tuple-element.63, f32[2,1536]{1,0:T(2,128)S(1)} %copy-done.41, u8[980,1536]{1,0:T(8,128)(4,1)S(1)} %get-tuple-element.18, u8[980,1536]{1,0:T(8,128)(4,1)S(1)} %get-tuple-element.17), kind=kLoop, calls=%fused_computation.14 | loop fusion | flops 213749760 | bytes 33128448 | tf_op jit(solution)/shard_map/convert_element_type | solution.py:180
  233.3 4.4 add_convert_fusion.1
  240.2 3.7 copy.80
  243.8 4.8 all-to-all-start.1
  251.0 17.0 %all-to-all-done.1 = bf16[4,2,245,384]{3,1,2,0:T(2,128)(2,1)} async-done(((bf16[4,2,245,384]{3,1,2,0:T(2,128)(2,1)}), bf16[4,2,245,384]{3,1,2,0:T(2,128)(2,1)}, u32[]{:S(2)}, u32[]{:S(2)}) %all-to-all-start.1) | async-done | bytes 1505312 | tf_op jit(solution)/shard_map/all_to_all | solution.py:189
  273.7 6.9 fusion.62
  280.7 6.0 fusion.51
  289.7 3.7 copy.82
  293.4 4.5 all-to-all-start.2
  299.8 17.5 %all-to-all-done.2 = bf16[4,2,245,384]{3,1,2,0:T(2,128)(2,1)} async-done(((bf16[4,2,245,384]{3,1,2,0:T(2,128)(2,1)}), bf16[4,2,245,384]{3,1,2,0:T(2,128)(2,1)}, u32[]{:S(2)}, u32[]{:S(2)}) %all-to-all-start.2) | async-done | bytes 1505312 | tf_op jit(solution)/shard_map/all_to_all | solution.py:192
  317.3 14.5 %fusion.111 = (bf16[2,1536]{1,0:T(2,128)(2,1)S(1)}, bf16[2,980,1536]{2,1,0:T(8,128)(2,1)}) fusion(f32[2,980,1536]{2,1,0:T(8,128)} %get-tuple-element.52, bf16[2,1536,384]{2,1,0:T(8,128)(2,1)} %param.33, bf16[2,980,384]{2,0,1:T(2,128)(2,1)} %bitcast.16, f32[2,980,1536]{2,1,0:T(8,128)} %get-tuple-element.63, f32[2,1536]{1,0:T(2,128)S(1)} %copy-done.41), kind=kOutput, calls=%fused_computation.177 | convolution fusion | flops 2360275968 | bytes 33988608 | tf_op jit(solution)/shard_map/erd,efd->erf/dot_general | solution.py:198
  334.5 21.9 %all-reduce.2 = (bf16[2,1536]{1,0:T(2,128)(2,1)S(1)}, bf16[2,384]{1,0:T(2,128)(2,1)S(1)}) all-reduce(bf16[2,1536]{1,0:T(2,128)(2,1)S(1)} %get-tuple-element.72, bf16[2,384]{1,0:T(2,128)(2,1)S(1)} %bitcast_reduce_fusion), channel_id=1, replica_groups=mesh['dp'=8,'expert'=4] {'dp'}, use_global_device_ids=true, to_apply=%region_36.37 | all-reduce | flops 3840 | bytes 15360 | tf_op jit(solution)/shard_map/psum | solution.py:300
  357.6 7.1 %convolution_convert_fusion.3 = bf16[2,980,384]{2,1,0:T(8,128)(2,1)} fusion(bf16[2,980,1536]{2,1,0:T(8,128)(2,1)} %get-tuple-element.73, bf16[2,384,1536]{2,1,0:T(8,128)(2,1)S(1)} %copy-done), kind=kOutput, calls=%fused_computation.109 | convolution fusion | flops 2312862720 | bytes 9885696 | tf_op jit(solution)/shard_map/erf,edf->erd/dot_general | solution.py:207
  368.6 4.3 all-to-all-start.3
  373.0 8.2 %convolution_convert_fusion = bf16[2,1536,384]{2,1,0:T(8,128)(2,1)} fusion(bf16[2,980,1536]{2,1,0:T(8,128)(2,1)} %copy-done.14, bf16[2,980,384]{2,0,1:T(2,128)(2,1)} %bitcast.16), kind=kOutput, calls=%fused_computation.66 | convolution fusion | flops 2313289728 | bytes 9885696 | tf_op jit(solution)/shard_map/erf,erd->efd/dot_general | solution.py:194
  381.2 6.8 convolution_convert_fusion.1
  388.5 3.9 all-to-all-done.3
  395.6 5.2 fusion.1
  418.8 8.8 %reshape_reshape.8 = bf16[32,49,12,32]{3,2,0,1:T(8,128)(2,1)} reshape(bf16[8,2,2,7,7,384]{5,2,1,0,4,3:T(2,128)(2,1)} %copy.87) | data formatting | bytes 2408448 | tf_op jit(solution)/shard_map/reshape;reshape | solution.py:234
  427.6 8.5 %copy.88 = bf16[32,49,12,32]{1,3,2,0:T(8,128)(2,1)} copy(bf16[32,49,12,32]{3,2,0,1:T(8,128)(2,1)} %reshape_reshape.8) | data formatting | bytes 2408448 | tf_op jit(solution)/shard_map/reshape;reshape | solution.py:234
  436.1 13.8 %multiply_reduce_fusion = (f32[32,12,49]{2,1,0:T(8,128)S(1)}, f32[32,12,49,49]{2,3,1,0:T(8,128)}) fusion(f32[32,12,49,49]{2,3,1,0:T(8,128)} %copy-done.2, f32[32,12,49]{2,1,0:T(8,128)S(1)} %log_add_fusion, bf16[32,49,12,32]{1,3,2,0:T(8,128)(2,1)} %copy.88, bf16[32,49,1,12,32]{1,4,3,0,2:T(8,128)(2,1)} %copy.103), kind=kOutput, calls=%fused_computation.29 | convolution fusion | flops 61754112 | bytes 9934848 | tf_op jit(solution)/shard_map/wphd,wqhd->whpq/dot_general | solution.py:236
  449.9 9.7 %convert_reduce_fusion = (f32[12,49,49]{1,2,0:T(8,128)S(1)}, bf16[32,12,49,49]{2,3,1,0:T(8,128)(2,1)S(1)}) fusion(f32[32,12,49,49]{2,3,1,0:T(8,128)} %get-tuple-element.70, f32[32,12,49]{2,1,0:T(8,128)S(1)} %get-tuple-element.69, f32[32,12,49,49]{2,3,1,0:T(8,128)} %copy-done.2, f32[32,12,49]{2,1,0:T(8,128)S(1)} %log_add_fusion), kind=kLoop, calls=%fused_computation.27 | loop fusion | flops 5503092 | bytes 9485616 | tf_op jit(solution)/shard_map/reduce_sum | solution.py:249
  459.6 4.3 fusion.32
  467.3 8.9 %convert_bitcast_fusion = bf16[32,49,1,12,32]{1,4,3,0,2:T(8,128)(2,1)} fusion(bf16[32,49,12,32]{1,3,2,0:T(8,128)(2,1)S(1)} %copy-done.8, f32[32,12,49,49]{2,3,1,0:T(8,128)} %copy-done.2, f32[32,12,49]{2,1,0:T(8,128)S(1)} %log_add_fusion), kind=kOutput, calls=%fused_computation.80 | convolution fusion | flops 61453056 | bytes 6171648 | tf_op jit(solution)/shard_map/whpq,wphd->wqhd/dot_general | solution.py:239
  476.1 10.2 %pad_maximum_fusion = bf16[32,49,3,12,32]{1,4,3,0,2:T(8,128)(2,1)} fusion(bf16[32,49,1,12,32]{1,4,3,0,2:T(8,128)(2,1)} %convert_bitcast_fusion, bf16[32,49,1,12,32]{1,4,3,0,2:T(8,128)(2,1)} %fusion.32, bf16[32,49,1,12,32]{1,4,3,0,2:T(8,128)(2,1)} %fusion.31), kind=kLoop, calls=%fused_computation.34 | loop fusion | flops 3612672 | bytes 7225344 | tf_op jit(solution)/shard_map/stack | solution.py:259
  486.3 24.4 %copy.93 = bf16[32,49,3,12,32]{4,3,2,0,1:T(8,128)(2,1)} copy(bf16[32,49,3,12,32]{1,4,3,0,2:T(8,128)(2,1)} %pad_maximum_fusion) | data formatting | bytes 7225344 | tf_op jit(solution)/shard_map/stack | solution.py:259
  510.7 24.5 %convert_element_type.147 = bf16[8,2,2,7,7,1152]{5,2,1,0,4,3:T(2,128)(2,1)} reshape(bf16[32,49,3,12,32]{4,3,2,0,1:T(8,128)(2,1)} %copy.93) | data formatting | bytes 7225344 | tf_op jit(solution)/shard_map/convert_element_type | solution.py:262
  545.4 6.8 reshape.352
  553.3 5.0 fusion.101
  564.9 38.3 %all-reduce = (f32[384]{0:T(512)}, f32[384]{0:T(512)}, f32[384]{0:T(512)}, f32[384]{0:T(512)}, f32[169,12]{0,1:T(8,128)}, /*index=5*/f32[384]{0:T(512)}, f32[384]{0:T(512)}, f32[384]{0:T(512)}, f32[384,8]{0,1:T(8,128)}) all-reduce(f32[384]{0:T(512)S(1)} %get-tuple-element.21, ...), channel_id=1, replica_groups=mesh['dp'=8,'expert'=4] {'dp','expert'}, use_global_device_ids=true, to_apply=%region_17.18 | all-reduce | flops 7788 | bytes 62304 | tf_op jit(solution)/shard_map/psum | solution.py:282
  603.3 4.5 add_add_fusion.3
  607.7 4.7 convert_element_type.152
  614.9 82.3 %all-reduce.7.cloned.1.call-done = (f32[384,1152]{1,0:T(8,128)}, f32[384,384]{1,0:T(8,128)}) async-done(((f32[384,1152]{1,0:T(8,128)}, f32[384,384]{1,0:T(8,128)}), (f32[384,1152]{1,0:T(8,128)}, f32[384,384]{1,0:T(8,128)})) %all-reduce.7.cloned.1.call-update) | async-done | bytes 2359312 | tf_op jit(solution)/shard_map/psum | solution.py:282
  (188 shorter events, 117.8 us)
Async XLA Ops:
  7.2 182.8 %copy-start = (bf16[2,384,1536]{2,1,0:T(8,128)(2,1)S(1)}, bf16[2,384,1536]{2,1,0:T(8,128)(2,1)}, u32[]{:S(2)}) copy-start(bf16[2,384,1536]{2,1,0:T(8,128)(2,1)} %param.31) | copy-start | bytes 7077892
  9.0 3.2 copy-start.29
  25.8 4.8 copy-start.46
  35.2 3.0 copy-start.6
  101.9 8.8 %copy-start.26 = (f32[12,49,49]{1,2,0:T(8,128)S(1)}, f32[12,49,49]{1,2,0:T(8,128)}, u32[]{:S(2)}) copy-start(f32[12,49,49]{1,2,0:T(8,128)} %copy.73) | copy-start | bytes 345748
  116.9 4.8 copy-start.2
  116.9 4.8 copy-start.7
  142.8 1.6 copy-start.37
  142.8 1.6 copy-start.31
  144.7 4.7 copy-start.27
  144.7 4.7 copy-start.43
  149.4 4.2 copy-start.40
  149.4 4.2 copy-start.44
  152.2 1.4 copy-start.3
  163.8 26.1 %copy-start.41 = (f32[2,1536]{1,0:T(2,128)S(1)}, f32[2,1536]{1,0:T(2,128)}, u32[]{:S(2)}) copy-start(f32[2,1536]{1,0:T(2,128)} %param.32) | copy-start | bytes 36868
  190.0 10.0 %copy-start.24 = (bf16[4,2,245,384]{3,1,2,0:T(2,128)(2,1)}, bf16[4,2,245,384]{3,1,2,0:T(2,128)(2,1)S(1)}, u32[]{:S(2)}) copy-start(bf16[4,2,245,384]{3,1,2,0:T(2,128)(2,1)S(1)} %all_to_all.20) | copy-start | bytes 4515844
  200.0 33.3 %copy-start.45 = (bf16[2,1536,384]{2,1,0:T(8,128)(2,1)S(1)}, bf16[2,1536,384]{2,1,0:T(8,128)(2,1)}, u32[]{:S(2)}) copy-start(bf16[2,1536,384]{2,1,0:T(8,128)(2,1)} %param.33) | copy-start | bytes 7077892
  200.0 33.3 %copy-start.47 = (f32[2,384]{1,0:T(2,128)S(1)}, f32[2,384]{1,0:T(2,128)}, u32[]{:S(2)}) copy-start(f32[2,384]{1,0:T(2,128)} %param.34) | copy-start | bytes 9220
  230.8 2.5 copy-start.14
  240.2 8.4 %copy-start.36 = (f32[384,8]{0,1:T(8,128)S(1)}, f32[384,8]{0,1:T(8,128)}, u32[]{:S(2)}) copy-start(f32[384,8]{0,1:T(8,128)} %param.30) | copy-start | bytes 36868
  243.8 24.2 %all-to-all-start.1 = ((bf16[4,2,245,384]{3,1,2,0:T(2,128)(2,1)}), bf16[4,2,245,384]{3,1,2,0:T(2,128)(2,1)}, u32[]{:S(2)}, u32[]{:S(2)}) async-start(bf16[4,2,245,384]{3,1,2,0:T(2,128)(2,1)} %copy.80), calls=%async_computation.1 | async-start | bytes 3010560 | tf_op jit(solution)/shard_map/all_to_all | solution.py:189
  273.7 7.0 copy-start.17
  293.4 23.9 %all-to-all-start.2 = ((bf16[4,2,245,384]{3,1,2,0:T(2,128)(2,1)}), bf16[4,2,245,384]{3,1,2,0:T(2,128)(2,1)}, u32[]{:S(2)}, u32[]{:S(2)}) async-start(bf16[4,2,245,384]{3,1,2,0:T(2,128)(2,1)} %copy.82), calls=%async_computation.2 | async-start | bytes 3010560 | tf_op jit(solution)/shard_map/all_to_all | solution.py:192
  368.6 23.8 %all-to-all-start.3 = ((bf16[4,2,245,384]{3,1,2,0:T(2,128)(2,1)}), bf16[4,2,245,384]{3,1,2,0:T(2,128)(2,1)}, u32[]{:S(2)}, u32[]{:S(2)}) async-start(bf16[4,2,245,384]{3,1,2,0:T(2,128)(2,1)} %copy.84), calls=%async_computation.3 | async-start | bytes 3010560 | tf_op jit(solution)/shard_map/all_to_all | solution.py:218
  372.9 8.3 %copy-start.25 = (bf16[4,2,245,384]{3,1,2,0:T(2,128)(2,1)S(1)}, bf16[4,2,245,384]{3,1,2,0:T(2,128)(2,1)}, u32[]{:S(2)}) copy-start(bf16[4,2,245,384]{3,1,2,0:T(2,128)(2,1)} %copy-done.24) | copy-start | bytes 4515844
  373.0 234.8 %all-reduce.9.cloned.1.call-start = ((), (), s32[]{:S(2)}) async-start(), calls=%async_computation.5 | async-start | bytes 9437184 | tf_op jit(solution)/shard_map/psum | solution.py:299
  388.0 309.1 %all-reduce.7.cloned.1.call-start = ((), (), s32[]{:S(2)}) async-start(), calls=%async_computation.4 | async-start | bytes 4718592 | tf_op jit(solution)/shard_map/psum | solution.py:282
  395.6 5.2 copy-start.4
  400.7 3.2 copy-start.22
  404.0 3.4 copy-start.18
  405.9 1.4 copy-start.11
  449.9 9.7 %copy-start.9 = (bf16[32,49,1,12,32]{1,4,3,0,2:T(8,128)(2,1)S(1)}, bf16[32,49,1,12,32]{1,4,3,0,2:T(8,128)(2,1)}, u32[]{:S(2)}) copy-start(bf16[32,49,1,12,32]{1,4,3,0,2:T(8,128)(2,1)} %copy.104) | copy-start | bytes 3612676
  459.6 4.3 copy-start.10
  463.9 3.4 copy-start.8
  545.4 6.8 copy-start.39
  545.4 7.9 %copy-start.5 = (bf16[1568,384]{1,0:T(8,128)(2,1)S(1)}, bf16[1568,384]{1,0:T(8,128)(2,1)}, u32[]{:S(2)}) copy-start(bf16[1568,384]{1,0:T(8,128)(2,1)} %param.19) | copy-start | bytes 3612676
  545.4 7.9 %copy-start.30 = (f32[1568]{0:T(1024)S(1)}, f32[1568]{0:T(1024)}, u32[]{:S(2)}) copy-start(f32[1568]{0:T(1024)} %copy-done.29) | copy-start | bytes 18820
  545.4 7.9 %copy-start.42 = (f32[384]{0:T(512)S(1)}, f32[384]{0:T(512)}, u32[]{:S(2)}) copy-start(f32[384]{0:T(512)} %param.20) | copy-start | bytes 4612
  553.3 5.1 copy-start.35
  553.3 5.1 copy-start.16
  553.3 5.1 copy-start.20
  558.3 3.0 copy-start.13
  558.4 1.8 copy-start.33
  558.4 3.1 copy-start.21
  558.4 3.1 copy-start.48
  607.7 4.7 copy-start.23
  612.4 88.5 %copy-start.1 = (bf16[2,384,1536]{2,1,0:T(8,128)(2,1)S(1)}, bf16[2,384,1536]{2,1,0:T(8,128)(2,1)}, u32[]{:S(2)}) copy-start(bf16[2,384,1536]{2,1,0:T(8,128)(2,1)} %param.31) | copy-start | bytes 7077892
  697.2 2.9 copy-start.28
  (6 other events, 5.0 us)
Sparse Core Ops, SparseCore 0:
  388.1 167.6 all-reduce.8
  565.0 132.0 all-reduce.6
where the time goes:
time: 715 us; the launch traced here: 708 us
  local copies, waits for them, and re-layouts  240 us (34%)
  matrix products  146 us (20%)
  waiting for transfers between devices  121 us (17%)
  other arithmetic  87.7 us (12%)
  blocking collectives  83.8 us (12%)
  between operations  15.1 us (2%)
  starting transfers between devices  14.1 us (2%)
    psum x1, waiting for transfers between devices, shards(): lax.psum((grad_ln1_gain, grad_ln1_bias, grad_qkv_weight, grad_q_bias, gra...  82.3 us
    unnamed x103, local copies, waits for them, and re-layouts  39.9 us
    psum x1, blocking collectives, shards(): lax.psum((grad_ln1_gain, grad_ln1_bias, grad_qkv_weight, grad_q_bias, gra...  38.3 us
    convert_element_type x1, other arithmetic, shards(): hidden_low = exact_gelu(hidden_pre).astype(jnp.bfloat16)  30.8 us
    convert_element_type x1, local copies, waits for them, and re-layouts, shards(): grad_projected = shift_out(stacked.astype(jnp.bfloat16), image_count)  24.5 us
    another operation x1, local copies, waits for them, and re-layouts, shards(): jnp.stack([grad_queries, grad_keys, grad_values], axis=2)  24.4 us
    all_to_all x1, blocking collectives, shards(): lax.all_to_all(outgoing, 'expert', split_axis=0, concat_axis=0, tiled=True)  23.5 us
    another operation x1, local copies, waits for them, and re-layouts, shards(): shift_in(projected, image_count).reshape(-1, window_cells, 3, HEADS, HEAD)  23.3 us
  transfers between devices with their start and end apart: 5, of which 4 were waited for; matrix products, arithmetic and copies ran while one was open for 28% of the time, Pallas kernels for 0%

commit v1 on v0

v1 whole, which is shorter than its diff:
```python
from functools import partial

import jax
import jax.numpy as jnp
import numpy as np
from jax import lax
from jax.experimental import pallas as pl
from jax.experimental.pallas import tpu as pltpu
from jax.sharding import PartitionSpec as P

D = 384
HEADS = 12
HEAD = 32
FF = 1536
EXPERTS = 8
WINDOW = 7
SIDE = 14
SHIFT = 3
CAP = 245
CELLS = WINDOW * WINDOW
IMAGE = SIDE * SIDE
TABLE = (2 * WINDOW - 1) ** 2

ROWS = 64
SLOTS = 256
FRAME = 4 * ROWS
SPAN = 208
GROUP = 4
GROUPS = HEADS // GROUP
LANES = GROUP * HEAD
WIDE = GROUP * ROWS

EPSILON = 1e-05
MASK_NEG = -100.0
SCALE = HEAD ** (-0.5)
HIGHEST = lax.Precision.HIGHEST
F32 = jnp.float32
BF16 = jnp.bfloat16


def source_cells():
    source = np.full((FRAME, 1), -1000, np.int32)
    for row in range(FRAME):
        window, cell = divmod(row, ROWS)
        if cell < CELLS:
            down = (window // 2) * WINDOW + cell // WINDOW
            across = (window % 2) * WINDOW + cell % WINDOW
            source[row, 0] = ((down + SHIFT) % SIDE) * SIDE + (across + SHIFT) % SIDE
    return source


def window_masks():
    places = np.arange(SIDE)
    bands = (places >= SIDE - WINDOW).astype(np.int32) + (places >= SIDE - SHIFT)
    masks = np.zeros((4, ROWS, ROWS), np.float32)
    for window in range(4):
        rows = bands[(window // 2) * WINDOW : (window // 2 + 1) * WINDOW]
        cols = bands[(window % 2) * WINDOW : (window % 2 + 1) * WINDOW]
        labels = (rows[:, None] * 3 + cols[None, :]).reshape(-1)
        masks[window, :CELLS, :CELLS] = np.where(labels[:, None] != labels[None, :], MASK_NEG, 0.0)
    masks[:, CELLS:, :] = -1e30
    return np.tile(masks, (1, 1, GROUP))


def offset_onehot():
    hot = np.zeros((TABLE, ROWS, ROWS), np.float32)
    for q in range(CELLS):
        for p in range(CELLS):
            entry = (p // WINDOW - q // WINDOW + WINDOW - 1) * (2 * WINDOW - 1)
            entry += p % WINDOW - q % WINDOW + WINDOW - 1
            hot[entry, q, p] = 1.0
    return hot.reshape(TABLE, ROWS * ROWS)


def mm(left, right):
    return jnp.dot(left, right, preferred_element_type=F32)


def mm_nt(left, right):
    return lax.dot_general(left, right, (((1,), (1,)), ((), ())), preferred_element_type=F32)


def mm_tn(left, right):
    return lax.dot_general(left, right, (((0,), (0,)), ((), ())), preferred_element_type=F32)


def permutation(source, offset, width):
    places = lax.broadcasted_iota(jnp.int32, (FRAME, width), 1)
    return jnp.where(source + offset == places, 1.0, 0.0).astype(BF16)


def normalize(values):
    center = values - jnp.mean(values, axis=-1, keepdims=True)
    inverse = lax.rsqrt(jnp.mean(center * center, axis=-1, keepdims=True) + EPSILON)
    return center * inverse, inverse


def normalize_pull(grad, hat, inverse, gain):
    scaled = grad * gain
    first = jnp.mean(scaled, axis=-1, keepdims=True)
    second = jnp.mean(scaled * hat, axis=-1, keepdims=True)
    return (scaled - first - hat * second) * inverse


def spread_heads(block):
    heads = lax.broadcasted_iota(jnp.int32, block.shape, 1) // HEAD
    return jnp.concatenate(
        [jnp.where(heads == h, block, jnp.zeros_like(block)) for h in range(GROUP)], axis=0
    )


def pick_heads(wide):
    heads = lax.broadcasted_iota(jnp.int32, (ROWS, LANES), 1) // HEAD
    picked = wide[:ROWS]
    for h in range(1, GROUP):
        picked = jnp.where(heads == h, wide[h * ROWS : (h + 1) * ROWS], picked)
    return picked


def image_span(image):
    offset = lax.rem(image * (IMAGE % 16), 16)
    return pl.multiple_of(image * IMAGE - offset, 16), offset


def split_three(values):
    high = values.astype(BF16)
    rest = values - high.astype(F32)
    middle = rest.astype(BF16)
    return high, middle, (rest - middle.astype(F32)).astype(BF16)


def forward_kernel(
    tokens_ref, grad_ref, route_ref, source_ref, gain1_ref, bias1_ref, qkv_ref, offset_ref, relative_ref,
    mask_ref, out_weight_ref, out_bias_ref, gain2_ref, bias2_ref, router_ref,
    projected_ref, weights_ref, attended_ref, residual_ref, rows_ref, place_ref, aux_ref,
):
    image = pl.program_id(0)
    start, offset = image_span(image)
    source = source_ref[...]
    order = permutation(source, offset, SPAN)
    inputs = mm(order, tokens_ref[pl.ds(start, SPAN), :])
    upstream = mm(order, grad_ref[pl.ds(start, SPAN), :])

    plain = permutation(source, 0, FRAME)
    route = route_ref[0]
    route_cols = mm_nt(plain, route)
    route_rows = mm_nt(route, plain)
    chosen_col = route_cols[:, 0:1]
    slot_col = route_cols[:, 1:2]
    place_row = jnp.where(
        route_rows[1:2] > 0.5, route_rows[0:1] * SLOTS + route_rows[1:2] - 1.0, -1.0
    )
    place_ref[0] = jnp.broadcast_to(place_row, (8, FRAME)).astype(jnp.int32)
    place_col = jnp.where(slot_col > 0.5, chosen_col * SLOTS + slot_col - 1.0, -1.0)

    hat, _ = normalize(inputs)
    normed = (hat * gain1_ref[...] + bias1_ref[...]).astype(BF16)
    projected_ref[...] = (mm(normed, qkv_ref[...]) + offset_ref[...]).astype(BF16)

    for window in range(4):
        rows = slice(window * ROWS, (window + 1) * ROWS)
        for group in range(GROUPS):
            cols = slice(group * LANES, (group + 1) * LANES)
            wide = slice(group * WIDE, (group + 1) * WIDE)
            queries = projected_ref[rows, group * LANES : (group + 1) * LANES]
            keys = projected_ref[rows, D + group * LANES : D + (group + 1) * LANES]
            values = projected_ref[rows, 2 * D + group * LANES : 2 * D + (group + 1) * LANES]
            scores = mm_nt(keys, spread_heads(queries)) * SCALE
            scores = scores + relative_ref[:, wide] + mask_ref[window]
            powers = jnp.exp(scores - jnp.max(scores, axis=0, keepdims=True))
            weights = (powers / jnp.sum(powers, axis=0, keepdims=True)).astype(BF16)
            place = (window * GROUPS + group) * ROWS
            weights_ref[place : place + ROWS, :] = weights
            attended_ref[rows, cols] = pick_heads(mm_tn(weights, values)).astype(BF16)

    residual = inputs + (mm(attended_ref[...], out_weight_ref[...]) + out_bias_ref[...])
    residual_ref[...] = residual
    hat, _ = normalize(residual)
    normed = (hat * gain2_ref[...] + bias2_ref[...]).astype(BF16)
    logits = sum(mm(normed, part) for part in split_three(router_ref[...]))
    logits = jnp.exp(logits - jnp.max(logits, axis=-1, keepdims=True))
    probs = logits / jnp.sum(logits, axis=-1, keepdims=True)
    experts = lax.broadcasted_iota(jnp.int32, (FRAME, EXPERTS), 1).astype(F32)
    gate = jnp.sum(jnp.where(experts == chosen_col, probs, 0.0), axis=-1, keepdims=True)
    rows_ref[:, :D] = normed
    rows_ref[:, D:] = (gate * upstream).astype(BF16)
    aux_ref[:, 0:EXPERTS] = probs
    aux_ref[:, EXPERTS : EXPERTS + 1] = gate
    aux_ref[:, EXPERTS + 1 : EXPERTS + 2] = place_col
    aux_ref[:, EXPERTS + 2 : EXPERTS + 3] = chosen_col


def dispatch_kernel(place_ref, rows_ref, out_ref):
    expert = pl.program_id(0)
    images = place_ref.shape[0]
    places = jnp.concatenate([place_ref[i, 0:1, :] for i in range(images)], axis=1)
    slots = lax.broadcasted_iota(jnp.int32, (SLOTS, places.shape[1]), 0) + expert * SLOTS
    hot = jnp.where(slots == places, 1.0, 0.0).astype(BF16)
    out_ref[0] = mm(hot, rows_ref[...]).astype(BF16)


TILE = 512


def expert_kernel(
    rows_ref, up_ref, up_bias_ref, down_ref, down_bias_ref,
    back_ref, grad_up_ref, grad_up_bias_ref, grad_down_ref, grad_down_bias_ref,
    up_sum, down_sum, up_bias_sum, down_bias_sum,
):
    member = pl.program_id(1)
    last = pl.num_programs(1) - 1

    @pl.when(member == 0)
    def _():
        up_sum[...] = jnp.zeros_like(up_sum)
        down_sum[...] = jnp.zeros_like(down_sum)
        up_bias_sum[...] = jnp.zeros_like(up_bias_sum)
        down_bias_sum[...] = jnp.zeros_like(down_bias_sum)

    inputs = rows_ref[0, 0, :, :D]
    grads = rows_ref[0, 0, :, D:]
    inputs_t = inputs.T
    grads_t = grads.T
    outs = jnp.zeros((SLOTS, D), F32)
    backs = jnp.zeros((SLOTS, D), F32)
    for tile in range(FF // TILE):
        at = slice(tile * TILE, (tile + 1) * TILE)
        pre = mm(inputs, up_ref[0, :, at]) + up_bias_ref[0, :, at]
        grad_hidden = mm_nt(grads, down_ref[0, at, :])
        share = 0.5 + 0.5 * lax.erf(pre * 0.7071067811865476)
        density = jnp.exp(pre * pre * -0.5) * 0.3989422804014327
        hidden = (pre * share).astype(BF16)
        grad_pre = (grad_hidden * (share + pre * density)).astype(BF16)
        outs += mm(hidden, down_ref[0, at, :])
        backs += mm_nt(grad_pre, up_ref[0, :, at])
        down_sum[:, at] += mm(grads_t, hidden)
        up_sum[:, at] += mm(inputs_t, grad_pre)
        up_bias_sum[:, at] += jnp.sum(grad_pre.astype(F32), axis=0, keepdims=True)
    down_bias_sum[...] += jnp.sum(grads.astype(F32), axis=0, keepdims=True)
    back_ref[0, 0, :, :D] = (outs + down_bias_ref[0]).astype(BF16)
    back_ref[0, 0, :, D:] = backs.astype(BF16)

    @pl.when(member == last)
    def _():
        grad_up_ref[0] = up_sum[...].astype(BF16)
        grad_down_ref[0] = down_sum[...].T.astype(BF16)
        grad_up_bias_ref[0] = up_bias_sum[...]
        grad_down_bias_ref[0] = down_bias_sum[...]


def backward_kernel(
    tokens_ref, grad_ref, source_ref, gain1_ref, bias1_ref, qkv_ref, out_weight_ref, gain2_ref, bias2_ref,
    router_ref, projected_ref, weights_ref, attended_ref, residual_ref, aux_ref, returned_ref,
    output_ref, grad_tokens_ref, grad_qkv_ref, grad_out_ref, totals_ref, grad_router_ref, small_ref,
    grad_projected,
):
    image = pl.program_id(0)

    @pl.when(image == 0)
    def _():
        for ref in (output_ref, grad_tokens_ref, grad_qkv_ref, grad_out_ref, totals_ref, grad_router_ref, small_ref):
            ref[...] = jnp.zeros_like(ref)

    start, offset = image_span(image)
    order = permutation(source_ref[...], offset, SPAN)
    inputs = mm(order, tokens_ref[pl.ds(start, SPAN), :])
    upstream = mm(order, grad_ref[pl.ds(start, SPAN), :])
    residual = residual_ref[...]
    aux = aux_ref[...]
    probs = aux[:, 0:EXPERTS]
    gate = aux[:, EXPERTS : EXPERTS + 1]
    place = aux[:, EXPERTS + 1 : EXPERTS + 2].astype(jnp.int32)
    chosen = aux[:, EXPERTS + 2 : EXPERTS + 3]

    slots = lax.broadcasted_iota(jnp.int32, (FRAME, EXPERTS * SLOTS), 1)
    hot = jnp.where(slots == place, 1.0, 0.0).astype(BF16)
    gathered = mm(hot, returned_ref[...])
    combined = gathered[:, :D]
    output = (residual + gate * combined).astype(BF16)
    output_ref[pl.ds(start, SPAN), :] += mm_tn(order, output).astype(BF16)

    hat2, inverse2 = normalize(residual)
    normed2 = (hat2 * gain2_ref[...] + bias2_ref[...]).astype(BF16)
    gate_grad = jnp.sum(upstream * combined, axis=-1, keepdims=True)
    experts = lax.broadcasted_iota(jnp.int32, (FRAME, EXPERTS), 1).astype(F32)
    grad_logits = gate_grad * gate * (jnp.where(experts == chosen, 1.0, 0.0) - probs)
    logits_high, logits_low, _ = split_three(grad_logits)
    grad_router_ref[...] += mm_tn(logits_high, normed2) + mm_tn(logits_low, normed2)
    router_high, router_low, _ = split_three(router_ref[...])
    grad_normed = (
        gathered[:, D:]
        + mm_nt(logits_high, router_high)
        + mm_nt(logits_low, router_high)
        + mm_nt(logits_high, router_low)
    )
    small_ref[0:1, :D] += jnp.sum(grad_normed * hat2, axis=0, keepdims=True)
    small_ref[1:2, :D] += jnp.sum(grad_normed, axis=0, keepdims=True)
    grad_residual = upstream + normalize_pull(grad_normed, hat2, inverse2, gain2_ref[...])
    mixed = grad_residual.astype(BF16)
    grad_out_ref[...] += mm_tn(attended_ref[...], mixed)
    small_ref[2:3, :D] += jnp.sum(mixed.astype(F32), axis=0, keepdims=True)
    grad_attended = mm_nt(mixed, out_weight_ref[...]).astype(BF16)

    for window in range(4):
        rows = slice(window * ROWS, (window + 1) * ROWS)
        for group in range(GROUPS):
            cols = slice(group * LANES, (group + 1) * LANES)
            wide = slice(group * WIDE, (group + 1) * WIDE)
            key_cols = slice(D + group * LANES, D + (group + 1) * LANES)
            value_cols = slice(2 * D + group * LANES, 2 * D + (group + 1) * LANES)
            keys = projected_ref[rows, key_cols]
            values = projected_ref[rows, value_cols]
            spread_queries = spread_heads(projected_ref[rows, cols])
            spread_grads = spread_heads(grad_attended[rows, cols])
            at = (window * GROUPS + group) * ROWS
            weights = weights_ref[at : at + ROWS, :]
            exact = weights.astype(F32)
            grad_weights = mm_nt(values, spread_grads)
            grad_scores = exact * (grad_weights - jnp.sum(exact * grad_weights, axis=0, keepdims=True))
            grad_scores = grad_scores.astype(BF16)
            totals_ref[:, wide] += grad_scores.astype(F32)
            grad_projected[rows, value_cols] = mm(weights, spread_grads).astype(BF16)
            grad_projected[rows, key_cols] = (mm(grad_scores, spread_queries) * SCALE).astype(BF16)
            grad_projected[rows, cols] = (pick_heads(mm_tn(grad_scores, keys)) * SCALE).astype(BF16)

    grads = grad_projected[...]
    hat1, inverse1 = normalize(inputs)
    normed1 = (hat1 * gain1_ref[...] + bias1_ref[...]).astype(BF16)
    grad_qkv_ref[...] += mm_tn(normed1, grads)
    small_ref[5:6, :] += jnp.sum(grads.astype(F32), axis=0, keepdims=True)
    grad_normed = mm_nt(grads, qkv_ref[...])
    small_ref[3:4, :D] += jnp.sum(grad_normed * hat1, axis=0, keepdims=True)
    small_ref[4:5, :D] += jnp.sum(grad_normed, axis=0, keepdims=True)
    grad_inputs = grad_residual + normalize_pull(grad_normed, hat1, inverse1, gain1_ref[...])
    high, low, _ = split_three(grad_inputs)
    grad_tokens_ref[pl.ds(start, SPAN), :] += mm_tn(order, high) + mm_tn(order, low)


def whole(shape):
    return pl.BlockSpec(shape, lambda *_: (0,) * len(shape))


def per_image(rows, columns):
    return pl.BlockSpec((rows, columns), lambda i: (i, 0))


def shards(
    tokens, ln1_gain, ln1_bias, qkv_weight, q_bias, v_bias, bias_table, out_weight, out_bias, ln2_gain, ln2_bias,
    router_weight, up_weight, up_bias, down_weight, down_bias, expert_of, slot_of, grad_output,
):
    members = lax.axis_size("expert")
    local = up_weight.shape[0]
    count = tokens.shape[0]
    images = count // IMAGE
    framed = images * FRAME
    params = pltpu.CompilerParams(dimension_semantics=("arbitrary",), vmem_limit_bytes=60 * 2**20)

    source = jnp.asarray(source_cells())
    masks = jnp.asarray(window_masks())
    hot = jnp.asarray(offset_onehot())
    relative = jnp.dot(bias_table.T, hot, precision=HIGHEST).reshape(HEADS, ROWS, ROWS)
    relative = relative.transpose(1, 0, 2).reshape(ROWS, HEADS * ROWS)
    offset = jnp.concatenate([q_bias, jnp.zeros_like(q_bias), v_bias])[None]
    route = jnp.stack([expert_of, slot_of + 1]).astype(BF16).reshape(2, images, IMAGE).transpose(1, 0, 2)
    route = jnp.pad(route, ((0, 0), (0, 6), (0, FRAME - IMAGE)))
    row = lambda v: v[None]

    projected, weights, attended, residual, rows, place, aux = pl.pallas_call(
        forward_kernel,
        grid=(images,),
        in_specs=[
            whole((count, D)), whole((count, D)), pl.BlockSpec((1, 8, FRAME), lambda i: (i, 0, 0)),
            whole((FRAME, 1)), whole((1, D)), whole((1, D)), whole((D, 3 * D)), whole((1, 3 * D)),
            whole((ROWS, HEADS * ROWS)), whole((4, ROWS, WIDE)), whole((D, D)), whole((1, D)), whole((1, D)),
            whole((1, D)), whole((D, EXPERTS)),
        ],
        out_specs=[
            per_image(FRAME, 3 * D), per_image(4 * GROUPS * ROWS, WIDE), per_image(FRAME, D), per_image(FRAME, D),
            per_image(FRAME, 2 * D), pl.BlockSpec((1, 8, FRAME), lambda i: (i, 0, 0)), per_image(FRAME, 128),
        ],
        out_shape=[
            jax.ShapeDtypeStruct((framed, 3 * D), BF16),
            jax.ShapeDtypeStruct((images * 4 * GROUPS * ROWS, WIDE), BF16),
            jax.ShapeDtypeStruct((framed, D), BF16),
            jax.ShapeDtypeStruct((framed, D), F32),
            jax.ShapeDtypeStruct((framed, 2 * D), BF16),
            jax.ShapeDtypeStruct((images, 8, FRAME), jnp.int32),
            jax.ShapeDtypeStruct((framed, 128), F32),
        ],
        compiler_params=params,
        name="forward",
    )(
        tokens, grad_output, route, source, row(ln1_gain), row(ln1_bias), qkv_weight, offset, relative, masks,
        out_weight, row(out_bias), row(ln2_gain), row(ln2_bias), router_weight,
    )

    sending = pl.pallas_call(
        dispatch_kernel,
        grid=(EXPERTS,),
        in_specs=[whole((images, 8, FRAME)), whole((framed, 2 * D))],
        out_specs=pl.BlockSpec((1, SLOTS, 2 * D), lambda e: (e, 0, 0)),
        out_shape=jax.ShapeDtypeStruct((EXPERTS, SLOTS, 2 * D), BF16),
        compiler_params=params,
        name="dispatch",
    )(place, rows)

    arrived = lax.all_to_all(
        sending.reshape(members, local, SLOTS, 2 * D), "expert", split_axis=0, concat_axis=0, tiled=True
    )
    per_block = pl.BlockSpec((1, 1, SLOTS, 2 * D), lambda j, m: (m, j, 0, 0))

    def per_expert(*shape):
        return pl.BlockSpec((1, *shape), lambda j, m: (j, 0, 0))

    back, grad_up, grad_up_bias, grad_down, grad_down_bias = pl.pallas_call(
        expert_kernel,
        grid=(local, members),
        in_specs=[per_block, per_expert(D, FF), per_expert(1, FF), per_expert(FF, D), per_expert(1, D)],
        out_specs=[per_block, per_expert(D, FF), per_expert(1, FF), per_expert(FF, D), per_expert(1, D)],
        out_shape=[
            jax.ShapeDtypeStruct((members, local, SLOTS, 2 * D), BF16),
            jax.ShapeDtypeStruct((local, D, FF), BF16),
            jax.ShapeDtypeStruct((local, 1, FF), F32),
            jax.ShapeDtypeStruct((local, FF, D), BF16),
            jax.ShapeDtypeStruct((local, 1, D), F32),
        ],
        scratch_shapes=[
            pltpu.VMEM((D, FF), F32), pltpu.VMEM((D, FF), F32), pltpu.VMEM((1, FF), F32), pltpu.VMEM((1, D), F32),
        ],
        compiler_params=pltpu.CompilerParams(
            dimension_semantics=("arbitrary", "arbitrary"), vmem_limit_bytes=60 * 2**20
        ),
        name="experts",
    )(arrived, up_weight, up_bias[:, None], down_weight, down_bias[:, None])

    returned = lax.all_to_all(back, "expert", split_axis=0, concat_axis=0, tiled=True)
    returned = returned.reshape(EXPERTS * SLOTS, 2 * D)
    grad_up, grad_down = lax.psum((grad_up, grad_down), "dp")

    output, grad_tokens, grad_qkv, grad_out, totals, grad_router, small = pl.pallas_call(
        backward_kernel,
        grid=(images,),
        in_specs=[
            whole((count, D)), whole((count, D)), whole((FRAME, 1)), whole((1, D)), whole((1, D)),
            whole((D, 3 * D)), whole((D, D)), whole((1, D)), whole((1, D)), whole((D, EXPERTS)),
            per_image(FRAME, 3 * D), per_image(4 * GROUPS * ROWS, WIDE), per_image(FRAME, D), per_image(FRAME, D),
            per_image(FRAME, 128), whole((EXPERTS * SLOTS, 2 * D)),
        ],
        out_specs=[
            whole((count, D)), whole((count, D)), whole((D, 3 * D)), whole((D, D)),
            whole((ROWS, HEADS * ROWS)), whole((EXPERTS, D)), whole((8, 3 * D)),
        ],
        out_shape=[
            jax.ShapeDtypeStruct((count, D), BF16),
            jax.ShapeDtypeStruct((count, D), F32),
            jax.ShapeDtypeStruct((D, 3 * D), F32),
            jax.ShapeDtypeStruct((D, D), F32),
            jax.ShapeDtypeStruct((ROWS, HEADS * ROWS), F32),
            jax.ShapeDtypeStruct((EXPERTS, D), F32),
            jax.ShapeDtypeStruct((8, 3 * D), F32),
        ],
        scratch_shapes=[pltpu.VMEM((FRAME, 3 * D), BF16)],
        compiler_params=params,
        name="backward",
    )(
        tokens, grad_output, source, row(ln1_gain), row(ln1_bias), qkv_weight, out_weight, row(ln2_gain),
        row(ln2_bias), router_weight, projected, weights, attended, residual, aux, returned,
    )

    totals = totals.reshape(ROWS, HEADS, ROWS).transpose(1, 0, 2).reshape(HEADS, ROWS * ROWS)
    grad_table = lax.dot_general(totals, hot, (((1,), (1,)), ((), ())), precision=HIGHEST)
    grad_qkv, grad_out = lax.psum((grad_qkv.astype(BF16), grad_out.astype(BF16)), ("dp", "expert"))
    grad_table, grad_router, small = lax.psum((grad_table, grad_router, small), ("dp", "expert"))
    grad_up_bias, grad_down_bias = lax.psum((grad_up_bias, grad_down_bias), "dp")
    return (
        output,
        grad_tokens,
        small[3, :D],
        small[4, :D],
        grad_qkv.astype(F32),
        small[5, :D],
        small[5, 2 * D :],
        grad_table.T,
        grad_out.astype(F32),
        small[2, :D],
        small[0, :D],
        small[1, :D],
        grad_router.T,
        grad_up.astype(F32),
        grad_up_bias[:, 0],
        grad_down.astype(F32),
        grad_down_bias[:, 0],
    )


def solution(mesh):
    tokens = P(("dp", "expert"), None)
    expert = P("expert", None, None)
    expert_bias = P("expert", None)
    routes = P(("dp", "expert"))
    return jax.shard_map(
        shards,
        mesh=mesh,
        in_specs=(
            tokens, P(), P(), P(), P(), P(), P(), P(), P(), P(), P(), P(), expert, expert_bias, expert, expert_bias,
            routes, routes, tokens,
        ),
        out_specs=(
            tokens, tokens, P(), P(), P(), P(), P(), P(), P(), P(), P(), P(), P(), expert, expert_bias, expert,
            expert_bias,
        ),
        check_vma=False,
    )
```

time: 715 us -> 548 us (0.77)
  local copies, waits for them, and re-layouts: 240 us -> 17 us
  matrix products: 146 us -> 5.95 us
  waiting for transfers between devices: 121 us -> 254 us
  Pallas kernels: 0 us -> 115 us
  other arithmetic: 87.7 us -> 17.9 us
  blocking collectives: 83.8 us -> 120 us
  starting transfers between devices: 14.1 us -> 4.39 us
    dot_general x27 -> x2, matrix products: 146 us -> 5.95 us  [the longest x1 3.62 us: shards(): jnp.dot(bias_table.T, hot, precision=HIGHEST).reshape(HEADS, ROWS, ROWS)]
    psum x2, waiting for transfers between devices: 82.3 us -> 217 us  [the longest x1 169 us: shards(): grad_up, grad_down = lax.psum((grad_up, grad_down), 'dp')]
    pallas_call x0 -> x4, Pallas kernels: none -> 115 us  [the longest x1 52.4 us: shards(): pl.pallas_call(backward_kernel, grid=(images,), in_specs=[whole((count, D...]
    another operation x5 -> x2, local copies, waits for them, and re-layouts: 65 us -> 0.19 us  [shards(): jnp.stack([expert_of, slot_of + 1]).astype(BF16).reshape(2, images, IMAGE)]
    convert_element_type x3 -> x0, local copies, waits for them, and re-layouts: 42.5 us -> none  [the longest x1 24.5 us: shards(): grad_projected = shift_out(stacked.astype(jnp.bfloat16), image_count)]
    unnamed x103 -> x25, local copies, waits for them, and re-layouts: 39.9 us -> 3.29 us
    reshape x12 -> x5, local copies, waits for them, and re-layouts: 39.9 us -> 3.38 us  [the longest x2 2.18 us: shards(): totals.reshape(ROWS, HEADS, ROWS).transpose(1, 0, 2)]
    reduce_sum x12 -> x0, other arithmetic: 26.9 us -> none  [the longest x1 9.7 us: shards(): score_totals = jnp.sum(grad_scores_low.astype(jnp.float32), axis=0)]
  transfers between devices with their start and end apart: 5 -> 3, of which waited for: 4 -> 3; matrix products, arithmetic and copies ran while one was open for 28% -> 2% of each run, Pallas kernels for 0% -> 0%
where the time goes in v1:
time: 548 us; the launch traced here: 547 us
  waiting for transfers between devices  254 us (46%)
  blocking collectives  120 us (22%)
  Pallas kernels  115 us (21%)
  other arithmetic  17.9 us (3%)
  local copies, waits for them, and re-layouts  17 us (3%)
  between operations  14.2 us (3%)
  matrix products  5.95 us (1%)
    psum x1, waiting for transfers between devices, shards(): grad_up, grad_down = lax.psum((grad_up, grad_down), 'dp')  169 us
    pallas_call x1, Pallas kernels, shards(): pl.pallas_call(backward_kernel, grid=(images,), in_specs=[whole((count, D...  52.4 us
    psum x1, waiting for transfers between devices, shards(): lax.psum((grad_qkv.astype(BF16), grad_out.astype(BF16)), ('dp', 'expert'))  48.4 us
    all_to_all x1, blocking collectives, shards(): lax.all_to_all(back, 'expert', split_axis=0, concat_axis=0, tiled=True)  42.3 us
    psum x1, blocking collectives, shards(): lax.psum((grad_up_bias, grad_down_bias), 'dp')  39.1 us
    psum x1, blocking collectives, shards(): lax.psum((grad_table, grad_router, small), ('dp', 'expert'))  38.4 us
    all_to_all x1, waiting for transfers between devices, shards(): lax.all_to_all(sending.reshape(members, local, SLOTS, 2 * D), 'expert', s...  35.8 us
    pallas_call x1, Pallas kernels, shards(): pl.pallas_call(expert_kernel, grid=(local, members), in_specs=[per_block,...  28 us
  transfers between devices with their start and end apart: 3, of which 3 were waited for; matrix products, arithmetic and copies ran while one was open for 2% of the time, Pallas kernels for 0%

profile of v1, /device:TPU:0, one launch (start us, length us, event | category | flops | bytes accessed | tf_op | source)
XLA Modules:
  0.0 547.4 jit_solution(17456918439517943206)
XLA Ops:
  7.2 0.0 copy-start
  7.2 1.3 broadcast_in_dim.31.gain1_ref
  8.5 1.2 broadcast_in_dim.32.bias1_ref
  9.7 1.2 broadcast_in_dim.33.gain2_ref
  10.9 1.2 broadcast_in_dim.34.bias2_ref
  12.2 1.2 broadcast_in_dim.37.out_bias_ref
  13.4 0.7 convert.8
  14.1 0.1 stack.12
  14.2 0.7 add_convert_fusion
  14.9 0.1 stack.13
  15.0 0.7 pad_maximum_fusion
  15.8 0.6 broadcast_in_dim.36.offset_ref
  16.4 1.5 copy.46.router_ref
  17.9 3.6 convolution_bitcast_fusion
  21.5 0.2 reshape.59
  21.6 0.2 copy.53
  21.9 0.8 reshape.60.relative_ref
  22.7 0.6 pad.4.route_ref
  23.4 23.6 %forward.1 = (bf16[2048,1152]{1,0:T(8,128)(2,1)}, bf16[6144,256]{1,0:T(8,128)(2,1)}, bf16[2048,384]{1,0:T(8,128)(2,1)}, f32[2048,384]{1,0:T(8,128)}, bf16[2048,7...) custom-call(bf16[1568,384]{1,0:T(8,128)(2,1)} %tokens_ref.3, bf16[1568,384]{1,0:T(8,128)(2,1)} %grad_ref.3, ...), custom_call_target="tpu_custom_call" | custom-call | tf_op jit(solution)/shard_map/forward/pallas_call | solution.py:368
  47.0 10.7 %dispatch.1 = bf16[8,256,768]{2,1,0:T(8,128)(2,1)} custom-call(s32[8,8,256]{2,1,0:T(8,128)} %get-tuple-element.41.place_ref, bf16[2048,768]{1,0:T(8,128)(2,1)} %get-tuple-element.42.rows_ref), custom_call_target="tpu_custom_call" | custom-call | tf_op jit(solution)/shard_map/dispatch/pallas_call | solution.py:397
  57.7 4.3 all-to-all-start
  62.1 0.6 broadcast_in_dim.39.down_bias_ref
  62.7 0.6 broadcast_in_dim.38.up_bias_ref
  63.3 35.8 %all-to-all-done.rows_ref = bf16[4,2,256,768]{3,2,1,0:T(8,128)(2,1)S(1)} async-done(((bf16[4,2,256,768]{3,2,1,0:T(8,128)(2,1)}), bf16[4,2,256,768]{3,2,1,0:T(8,128)(2,1)S(1)}, u32[]{:S(2)}, u32[]{:S(2)}) %all-to-all-start) | async-done | bytes 3145760 | tf_op jit(solution)/shard_map/all_to_all | solution.py:407
  99.0 1.7 copy-done.2
  100.7 28.0 %experts.1 = (bf16[4,2,256,768]{3,2,1,0:T(8,128)(2,1)}, bf16[2,384,1536]{2,1,0:T(8,128)(2,1)}, f32[2,1,1536]{2,1,0:T(1,128)}, bf16[2,1536,384]{2,1,0:T(8,128)(2,1)}, f32[2,1,384]{2,1,0:T(1,128)}) custom-call(bf16[4,2,256,768]{3,2,1,0:T(8,128)(2,1)} %copy-done.2, bf16[2,384,1536]{2,1,0:T(8,128)(2,1)} %up_ref.1, f32[2,1,1536]{2,1,0:T(1,128)} %broadcast_in_dim.38.up_bias_ref, ...), custom_call_target="tpu_custom_call" | custom-call | tf_op jit(solution)/shard_map/experts/pallas_call | solution.py:415
  128.7 42.3 %all_to_all.10 = bf16[4,2,256,768]{3,2,1,0:T(8,128)(2,1)} all-to-all(bf16[4,2,256,768]{3,2,1,0:T(8,128)(2,1)} %get-tuple-element.43), channel_id=1, replica_groups=mesh['dp'=8,'expert'=4] {'expert'}, dimensions={0} | all-to-all | bytes 6291456 | tf_op jit(solution)/shard_map/all_to_all | solution.py:436
  171.0 52.4 %backward.1 = (bf16[1568,384]{1,0:T(8,128)(2,1)}, f32[1568,384]{1,0:T(8,128)}, f32[384,1152]{1,0:T(8,128)}, f32[384,384]{1,0:T(8,128)}, f32[64,768]{1,0:T(8,128)}, /*index=5*/f32[8,384]{1,0:T(8,128)}, f32[8,1152]{1,0:T(8,128)}) custom-call(bf16[1568,384]{1,0:T(8,128)(2,1)} %tokens_ref.3, bf16[1568,384]{1,0:T(8,128)(2,1)} %grad_ref.3, ...), custom_call_target="tpu_custom_call" | custom-call | tf_op jit(solution)/shard_map/backward/pallas_call | solution.py:440
  223.3 1.8 convert_element_type.24
  225.2 2.5 convert_element_type.22
  227.6 0.0 all-reduce.8.cloned.1.call-update
  227.7 0.0 all-reduce.10.cloned.1.call-start
  227.7 0.0 copy-start.3
  227.7 0.7 all-reduce.10.cloned.1.call-update
  228.5 39.1 %all-reduce.2 = (f32[2,1536]{1,0:T(2,128)}, f32[2,384]{1,0:T(2,128)}) all-reduce(f32[2,1536]{1,0:T(2,128)S(1)} %bitcast.25, f32[2,384]{1,0:T(2,128)S(1)} %bitcast.27), channel_id=1, replica_groups=mesh['dp'=8,'expert'=4] {'dp'}, use_global_device_ids=true, to_apply=%region_6.7 | all-reduce | flops 3840 | bytes 30720 | tf_op jit(solution)/shard_map/psum | solution.py:474
  267.6 1.0 reshape.63
  268.6 0.9 copy.47
  269.5 1.1 reshape.64
  270.7 2.3 fusion
  273.0 0.0 copy-done.5
  273.0 38.4 %all-reduce.1 = (f32[8,1152]{1,0:T(8,128)S(1)}, f32[169,12]{0,1:T(8,128)}, f32[384,8]{0,1:T(8,128)}) all-reduce(f32[8,1152]{1,0:T(8,128)S(1)} %copy-done.5, f32[169,12]{0,1:T(8,128)S(1)} %fusion, f32[384,8]{0,1:T(8,128)S(1)} %bitcast.26), channel_id=1, replica_groups=mesh['dp'=8,'expert'=4] {'dp','expert'}, use_global_device_ids=true, to_apply=%region_0.1 | all-reduce | flops 14316 | bytes 114528 | tf_op jit(solution)/shard_map/psum | solution.py:473
  311.4 0.6 slice_reduce_fusion
  312.0 48.4 %all-reduce.8.cloned.1.call-done = (bf16[384,1152]{1,0:T(8,128)(2,1)}, bf16[384,384]{1,0:T(8,128)(2,1)}) async-done(((bf16[384,1152]{1,0:T(8,128)(2,1)}, bf16[384,384]{1,0:T(8,128)(2,1)}), (bf16[384,1152]{1,0:T(8,128)(2,1)}, bf16[384,384]{1,0:T(8,128)(2,1)})) %all-reduce.8.cloned.1.call-update) | async-done | bytes 1179664 | tf_op jit(solution)/shard_map/psum | solution.py:472
  360.4 1.8 convert_element_type.25
  362.2 2.5 convert_element_type.23
  364.7 168.7 %all-reduce.10.cloned.1.call-done = (bf16[2,384,1536]{2,1,0:T(8,128)(2,1)}, bf16[2,1536,384]{2,1,0:T(8,128)(2,1)}) async-done(((bf16[2,384,1536]{2,1,0:T(8,128)(2,1)}, bf16[2,1536,384]{2,1,0:T(8,128)(2,1)}), (bf16[2,384,1536]{2,1,0:T(8,128)(2,1)}, bf16[2,1536,384]{2,1,0:T(8,128)(2,1)})) %all-reduce.10.cloned.1.call-update) | async-done | bytes 4718608 | tf_op jit(solution)/shard_map/psum | solution.py:438
  533.4 4.6 convert_element_type.26
  538.1 2.5 convert_element_type.27
  (23 shorter events, 0.1 us)
Async XLA Ops:
  7.2 10.7 %copy-start = (f32[169,12]{0,1:T(8,128)S(1)}, f32[169,12]{0,1:T(8,128)}, u32[]{:S(2)}) copy-start(f32[169,12]{0,1:T(8,128)} %param.28) | copy-start | bytes 24340
  57.7 4.4 copy-start.9
  57.7 4.9 copy-start.7
  57.7 41.3 %all-to-all-start = ((bf16[4,2,256,768]{3,2,1,0:T(8,128)(2,1)}), bf16[4,2,256,768]{3,2,1,0:T(8,128)(2,1)S(1)}, u32[]{:S(2)}, u32[]{:S(2)}) async-start(bf16[4,2,256,768]{3,2,1,0:T(8,128)(2,1)} %bitcast.22), calls=%async_computation | async-start | bytes 6291456 | tf_op jit(solution)/shard_map/all_to_all | solution.py:407
  62.1 298.3 %all-reduce.8.cloned.1.call-start = ((), (), s32[]{:S(2)}) async-start(), calls=%async_computation.2 | async-start | bytes 2359296 | tf_op jit(solution)/shard_map/psum | solution.py:472
  99.0 1.7 copy-start.2
  227.6 0.8 copy-start.10
  227.6 0.8 copy-start.8
  227.7 305.8 %all-reduce.10.cloned.1.call-start = ((), (), s32[]{:S(2)}) async-start(), calls=%async_computation.3 | async-start | bytes 9437184 | tf_op jit(solution)/shard_map/psum | solution.py:438
  227.7 42.9 %copy-start.3 = (f32[169,4096]{1,0:T(8,128)S(1)}, f32[169,4096]{1,0:T(8,128)}, u32[]{:S(2)}) copy-start(f32[169,4096]{1,0:T(8,128)} %constant.15.clone) | copy-start | bytes 8306692
  228.4 44.6 %copy-start.5 = (f32[8,1152]{1,0:T(8,128)S(1)}, f32[8,1152]{1,0:T(8,128)}, u32[]{:S(2)}) copy-start(f32[8,1152]{1,0:T(8,128)} %get-tuple-element.46) | copy-start | bytes 110596
  228.4 44.6 %copy-start.6 = (f32[8,384]{1,0:T(8,128)S(1)}, f32[8,384]{1,0:T(8,128)}, u32[]{:S(2)}) copy-start(f32[8,384]{1,0:T(8,128)} %get-tuple-element.50) | copy-start | bytes 36868
  533.4 4.7 copy-start.4
  538.1 2.5 copy-start.1
Sparse Core Ops, SparseCore 0:
  227.8 132.5 all-reduce.7
  364.5 168.9 all-reduce.9

commit v2 on v1

--- a/solution.py
+++ b/solution.py
@@ -204,8 +204,7 @@
 
 def expert_kernel(
     rows_ref, up_ref, up_bias_ref, down_ref, down_bias_ref,
-    back_ref, grad_up_ref, grad_up_bias_ref, grad_down_ref, grad_down_bias_ref,
-    up_sum, down_sum, up_bias_sum, down_bias_sum,
+    back_ref, chunks_ref, biases_ref, up_sum, down_sum, up_bias_sum, down_bias_sum,
 ):
     member = pl.program_id(1)
     last = pl.num_programs(1) - 1
@@ -242,23 +241,25 @@
 
     @pl.when(member == last)
     def _():
-        grad_up_ref[0] = up_sum[...].astype(BF16)
-        grad_down_ref[0] = down_sum[...].T.astype(BF16)
-        grad_up_bias_ref[0] = up_bias_sum[...]
-        grad_down_bias_ref[0] = down_bias_sum[...]
+        for tile in range(FF // D):
+            at = slice(tile * D, (tile + 1) * D)
+            chunks_ref[0, at, :] = up_sum[:, at].astype(BF16)
+            chunks_ref[1, at, :] = down_sum[:, at].T.astype(BF16)
+            biases_ref[tile : tile + 1, :] = up_bias_sum[:, at]
+        biases_ref[FF // D : FF // D + 1, :] = down_bias_sum[...]
+        biases_ref[FF // D + 1 :, :] = jnp.zeros((7 - FF // D, D), F32)
 
 
 def backward_kernel(
     tokens_ref, grad_ref, source_ref, gain1_ref, bias1_ref, qkv_ref, out_weight_ref, gain2_ref, bias2_ref,
     router_ref, projected_ref, weights_ref, attended_ref, residual_ref, aux_ref, returned_ref,
-    output_ref, grad_tokens_ref, grad_qkv_ref, grad_out_ref, totals_ref, grad_router_ref, small_ref,
-    grad_projected,
+    output_ref, grad_tokens_ref, shared_ref, totals_ref, small_ref, grad_projected, grad_qkv, grad_out,
 ):
     image = pl.program_id(0)
 
     @pl.when(image == 0)
     def _():
-        for ref in (output_ref, grad_tokens_ref, grad_qkv_ref, grad_out_ref, totals_ref, grad_router_ref, small_ref):
+        for ref in (output_ref, grad_tokens_ref, grad_qkv, grad_out, totals_ref, small_ref):
             ref[...] = jnp.zeros_like(ref)
 
     start, offset = image_span(image)
@@ -285,7 +286,7 @@
     experts = lax.broadcasted_iota(jnp.int32, (FRAME, EXPERTS), 1).astype(F32)
     grad_logits = gate_grad * gate * (jnp.where(experts == chosen, 1.0, 0.0) - probs)
     logits_high, logits_low, _ = split_three(grad_logits)
-    grad_router_ref[...] += mm_tn(logits_high, normed2) + mm_tn(logits_low, normed2)
+    small_ref[8:16, :] += mm_tn(logits_high, normed2) + mm_tn(logits_low, normed2)
     router_high, router_low, _ = split_three(router_ref[...])
     grad_normed = (
         gathered[:, D:]
@@ -293,12 +294,12 @@
         + mm_nt(logits_low, router_high)
         + mm_nt(logits_high, router_low)
     )
-    small_ref[0:1, :D] += jnp.sum(grad_normed * hat2, axis=0, keepdims=True)
-    small_ref[1:2, :D] += jnp.sum(grad_normed, axis=0, keepdims=True)
+    small_ref[0:1, :] += jnp.sum(grad_normed * hat2, axis=0, keepdims=True)
+    small_ref[1:2, :] += jnp.sum(grad_normed, axis=0, keepdims=True)
     grad_residual = upstream + normalize_pull(grad_normed, hat2, inverse2, gain2_ref[...])
     mixed = grad_residual.astype(BF16)
-    grad_out_ref[...] += mm_tn(attended_ref[...], mixed)
-    small_ref[2:3, :D] += jnp.sum(mixed.astype(F32), axis=0, keepdims=True)
+    grad_out[...] += mm_tn(attended_ref[...], mixed)
+    small_ref[2:3, :] += jnp.sum(mixed.astype(F32), axis=0, keepdims=True)
     grad_attended = mm_nt(mixed, out_weight_ref[...]).astype(BF16)
 
     for window in range(4):
@@ -326,14 +327,193 @@
     grads = grad_projected[...]
     hat1, inverse1 = normalize(inputs)
     normed1 = (hat1 * gain1_ref[...] + bias1_ref[...]).astype(BF16)
-    grad_qkv_ref[...] += mm_tn(normed1, grads)
-    small_ref[5:6, :] += jnp.sum(grads.astype(F32), axis=0, keepdims=True)
+    grad_qkv[...] += mm_tn(normed1, grads)
+    column_sums = jnp.sum(grads.astype(F32), axis=0, keepdims=True)
+    for third in range(3):
+        small_ref[5 + third : 6 + third, :] += column_sums[:, third * D : (third + 1) * D]
     grad_normed = mm_nt(grads, qkv_ref[...])
-    small_ref[3:4, :D] += jnp.sum(grad_normed * hat1, axis=0, keepdims=True)
-    small_ref[4:5, :D] += jnp.sum(grad_normed, axis=0, keepdims=True)
+    small_ref[3:4, :] += jnp.sum(grad_normed * hat1, axis=0, keepdims=True)
+    small_ref[4:5, :] += jnp.sum(grad_normed, axis=0, keepdims=True)
     grad_inputs = grad_residual + normalize_pull(grad_normed, hat1, inverse1, gain1_ref[...])
     high, low, _ = split_three(grad_inputs)
     grad_tokens_ref[pl.ds(start, SPAN), :] += mm_tn(order, high) + mm_tn(order, low)
+
+    @pl.when(image == pl.num_programs(0) - 1)
+    def _():
+        for third in range(3):
+            at = slice(third * D, (third + 1) * D)
+            shared_ref[at, :] = grad_qkv[:, at].astype(BF16)
+        shared_ref[3 * D :, :] = grad_out[...].astype(BF16)
+
+
+CHUNK = 4 * D
+STEP = 48
+MESH = pl.DeviceIdType.MESH
+
+
+def add_rows(left, left_at, right, right_at, out, out_at, count):
+    def body(i, carry):
+        here = i * STEP
+        total = left[pl.ds(pl.multiple_of(left_at + here, 16), STEP), :].astype(F32)
+        total = total + right[pl.ds(pl.multiple_of(right_at + here, 16), STEP), :].astype(F32)
+        out[pl.ds(pl.multiple_of(out_at + here, 16), STEP), :] = total.astype(out.dtype)
+        return carry
+
+    lax.fori_loop(0, count // STEP, body, 0)
+
+
+def partner(axis, stride):
+    index = lax.axis_index(axis)
+    bit = lax.rem(lax.div(index, stride), 2)
+    return bit, {axis: index + stride - 2 * stride * bit}
+
+
+class Halving:
+    def __init__(self, source, out, work, landing, sends, recvs, bits):
+        self.source, self.out, self.work, self.landing = source, out, work, landing
+        self.sends, self.recvs, self.bits = sends, recvs, bits
+        self.sizes = []
+        size = CHUNK
+        for _ in bits:
+            halved = size % 32 == 0 and (size // 2) % STEP == 0
+            size = size // 2 if halved else size
+            self.sizes.append((size, halved))
+        self.spreads = [k for k in reversed(range(len(bits))) if self.sizes[k][1]]
+        self.steps = len(bits) + len(self.spreads)
+
+    @staticmethod
+    def landing_rows(count):
+        rows, size = 0, CHUNK
+        for _ in range(count):
+            halved = size % 32 == 0 and (size // 2) % STEP == 0
+            size = size // 2 if halved else size
+            rows += size
+        return rows
+
+    def start(self, step):
+        count = len(self.bits)
+        if step == 0:
+            self.at, self.start_row, self.land = 0, 0, 0
+            self.held = []
+        if step < count:
+            size, halved = self.sizes[step]
+            bit, device = partner(*self.bits[step])
+            mine = self.source if step == 0 else self.work
+            if halved:
+                give, self.keep = self.at + (1 - bit) * size, self.at + bit * size
+                self.start_row = self.start_row + bit * size
+            else:
+                give = self.keep = self.at
+            self.held.append((self.start_row, size))
+            copy = pltpu.make_async_remote_copy(
+                src_ref=mine.at[pl.ds(pl.multiple_of(give, 16), size)],
+                dst_ref=self.landing.at[pl.ds(self.land, size)],
+                send_sem=self.sends.at[step], recv_sem=self.recvs.at[step], device_id=device, device_id_type=MESH,
+            )
+        else:
+            stage = self.spreads[step - count]
+            _, device = partner(*self.bits[stage])
+            start, size = self.held[stage]
+            rows = pl.ds(pl.multiple_of(start, 16), size)
+            copy = pltpu.make_async_remote_copy(
+                src_ref=self.out.at[rows], dst_ref=self.out.at[rows],
+                send_sem=self.sends.at[step], recv_sem=self.recvs.at[step], device_id=device, device_id_type=MESH,
+            )
+        copy.start()
+        self.copy = copy
+
+    def finish(self, step):
+        self.copy.wait()
+        count = len(self.bits)
+        if step >= count:
+            return
+        size, halved = self.sizes[step]
+        mine = self.source if step == 0 else self.work
+        if step == count - 1:
+            add_rows(mine, self.keep, self.landing, self.land, self.out, self.start_row, size)
+        elif step == 0:
+            add_rows(mine, self.keep, self.landing, self.land, self.work, 0, size)
+            self.at = 0
+        else:
+            add_rows(mine, self.keep, self.landing, self.land, self.work, self.keep, size)
+            self.at = self.keep
+        self.land += size
+
+
+class Doubling:
+    def __init__(self, source, out, landing, sends, recvs, bits):
+        self.source, self.out, self.landing = source, out, landing
+        self.sends, self.recvs, self.bits = sends, recvs, bits
+        self.steps = len(bits)
+
+    def start(self, step):
+        if step == 0:
+            self.out[...] = self.source[...]
+        _, device = partner(*self.bits[step])
+        self.copy = pltpu.make_async_remote_copy(
+            src_ref=self.out, dst_ref=self.landing.at[step],
+            send_sem=self.sends.at[step], recv_sem=self.recvs.at[step], device_id=device, device_id_type=MESH,
+        )
+        self.copy.start()
+
+    def finish(self, step):
+        self.copy.wait()
+        self.out[...] = self.out[...] + self.landing[step]
+
+
+def strides(size):
+    return [2**k for k in range(size.bit_length() - 1)]
+
+
+def copy_bits(copies):
+    low = len(strides(copies)) // 2
+    all_bits = [("dp", s) for s in strides(copies)]
+    return all_bits, all_bits[low : low + 1] + all_bits[:low] + all_bits[low + 1 :]
+
+
+def greet(bits):
+    barrier = pltpu.get_barrier_semaphore()
+    for bit in bits:
+        pl.semaphore_signal(barrier, inc=1, device_id=partner(*bit)[1], device_id_type=MESH)
+    pl.semaphore_wait(barrier, len(bits))
+
+
+def reduce_kernel(
+    copies, members, chunks_ref, biases_ref, shared_ref, small_ref,
+    chunks_out, biases_out, shared_out, small_out,
+    work, shared_work, landing, shared_landing, bias_landing, small_landing,
+    chunk_sends, chunk_recvs, shared_sends, shared_recvs, bias_sends, bias_recvs, small_sends, small_recvs,
+):
+    first, second = copy_bits(copies)
+    member_bits = [("expert", s) for s in strides(members)]
+    everyone = member_bits + first
+    greet(everyone)
+    streams = [
+        Doubling(small_ref, small_out, small_landing, small_sends, small_recvs, everyone),
+        Halving(shared_ref, shared_out, shared_work, shared_landing, shared_sends, shared_recvs, everyone),
+        Doubling(biases_ref, biases_out, bias_landing, bias_sends, bias_recvs, first),
+    ]
+    for c in range(chunks_ref.shape[0]):
+        streams.append(
+            Halving(
+                chunks_ref.at[c], chunks_out.at[c], work.at[c], landing.at[c], chunk_sends.at[c], chunk_recvs.at[c],
+                second if c % 4 == 3 else first,
+            )
+        )
+    run(streams)
+
+
+def run(streams):
+    at = [0] * len(streams)
+    for stream in streams:
+        stream.start(0)
+    while any(a < s.steps for a, s in zip(at, streams)):
+        for i, stream in enumerate(streams):
+            if at[i] < stream.steps:
+                stream.finish(at[i])
+                at[i] += 1
+                if at[i] < stream.steps:
+                    stream.start(at[i])
 
 
 def whole(shape):
@@ -412,17 +592,19 @@
     def per_expert(*shape):
         return pl.BlockSpec((1, *shape), lambda j, m: (j, 0, 0))
 
-    back, grad_up, grad_up_bias, grad_down, grad_down_bias = pl.pallas_call(
+    back, chunks, biases = pl.pallas_call(
         expert_kernel,
         grid=(local, members),
         in_specs=[per_block, per_expert(D, FF), per_expert(1, FF), per_expert(FF, D), per_expert(1, D)],
-        out_specs=[per_block, per_expert(D, FF), per_expert(1, FF), per_expert(FF, D), per_expert(1, D)],
+        out_specs=[
+            per_block,
+            pl.BlockSpec((2, CHUNK, D), lambda j, m: (j, 0, 0)),
+            pl.BlockSpec((8, D), lambda j, m: (j, 0)),
+        ],
         out_shape=[
             jax.ShapeDtypeStruct((members, local, SLOTS, 2 * D), BF16),
-            jax.ShapeDtypeStruct((local, D, FF), BF16),
-            jax.ShapeDtypeStruct((local, 1, FF), F32),
-            jax.ShapeDtypeStruct((local, FF, D), BF16),
-            jax.ShapeDtypeStruct((local, 1, D), F32),
+            jax.ShapeDtypeStruct((2 * local, CHUNK, D), BF16),
+            jax.ShapeDtypeStruct((8 * local, D), F32),
         ],
         scratch_shapes=[
             pltpu.VMEM((D, FF), F32), pltpu.VMEM((D, FF), F32), pltpu.VMEM((1, FF), F32), pltpu.VMEM((1, D), F32),
@@ -435,9 +617,8 @@
 
     returned = lax.all_to_all(back, "expert", split_axis=0, concat_axis=0, tiled=True)
     returned = returned.reshape(EXPERTS * SLOTS, 2 * D)
-    grad_up, grad_down = lax.psum((grad_up, grad_down), "dp")
-
-    output, grad_tokens, grad_qkv, grad_out, totals, grad_router, small = pl.pallas_call(
+
+    output, grad_tokens, shared, totals, small = pl.pallas_call(
         backward_kernel,
         grid=(images,),
         in_specs=[
@@ -447,19 +628,16 @@
             per_image(FRAME, 128), whole((EXPERTS * SLOTS, 2 * D)),
         ],
         out_specs=[
-            whole((count, D)), whole((count, D)), whole((D, 3 * D)), whole((D, D)),
-            whole((ROWS, HEADS * ROWS)), whole((EXPERTS, D)), whole((8, 3 * D)),
+            whole((count, D)), whole((count, D)), whole((CHUNK, D)), whole((ROWS, HEADS * ROWS)), whole((16, D)),
         ],
         out_shape=[
             jax.ShapeDtypeStruct((count, D), BF16),
             jax.ShapeDtypeStruct((count, D), F32),
-            jax.ShapeDtypeStruct((D, 3 * D), F32),
-            jax.ShapeDtypeStruct((D, D), F32),
+            jax.ShapeDtypeStruct((CHUNK, D), BF16),
             jax.ShapeDtypeStruct((ROWS, HEADS * ROWS), F32),
-            jax.ShapeDtypeStruct((EXPERTS, D), F32),
-            jax.ShapeDtypeStruct((8, 3 * D), F32),
-        ],
-        scratch_shapes=[pltpu.VMEM((FRAME, 3 * D), BF16)],
+            jax.ShapeDtypeStruct((16, D), F32),
+        ],
+        scratch_shapes=[pltpu.VMEM((FRAME, 3 * D), BF16), pltpu.VMEM((D, 3 * D), F32), pltpu.VMEM((D, D), F32)],
         compiler_params=params,
         name="backward",
     )(
@@ -469,27 +647,60 @@
 
     totals = totals.reshape(ROWS, HEADS, ROWS).transpose(1, 0, 2).reshape(HEADS, ROWS * ROWS)
     grad_table = lax.dot_general(totals, hot, (((1,), (1,)), ((), ())), precision=HIGHEST)
-    grad_qkv, grad_out = lax.psum((grad_qkv.astype(BF16), grad_out.astype(BF16)), ("dp", "expert"))
-    grad_table, grad_router, small = lax.psum((grad_table, grad_router, small), ("dp", "expert"))
-    grad_up_bias, grad_down_bias = lax.psum((grad_up_bias, grad_down_bias), "dp")
+    small = jnp.concatenate([small, jnp.pad(grad_table, ((0, 16 - HEADS), (0, D - TABLE)))])
+
+    copies = lax.axis_size("dp")
+    depth = len(strides(copies))
+    total = depth + len(strides(members))
+    rows_in = Halving.landing_rows
+    vmem = pl.BlockSpec(memory_space=pltpu.VMEM)
+    dma = pltpu.SemaphoreType.DMA
+    chunks, biases, shared, small = pl.pallas_call(
+        partial(reduce_kernel, copies, members),
+        in_specs=[vmem] * 4,
+        out_specs=[vmem] * 4,
+        out_shape=[jax.ShapeDtypeStruct(a.shape, a.dtype) for a in (chunks, biases, shared, small)],
+        scratch_shapes=[
+            pltpu.VMEM((2 * local, CHUNK // 2, D), BF16),
+            pltpu.VMEM((CHUNK // 2, D), BF16),
+            pltpu.VMEM((2 * local, rows_in(depth), D), BF16),
+            pltpu.VMEM((rows_in(total), D), BF16),
+            pltpu.VMEM((depth, *biases.shape), F32),
+            pltpu.VMEM((total, *small.shape), F32),
+            dma((2 * local, 2 * depth)), dma((2 * local, 2 * depth)), dma((2 * total,)), dma((2 * total,)),
+            dma((depth,)), dma((depth,)), dma((total,)), dma((total,)),
+        ],
+        compiler_params=pltpu.CompilerParams(
+            collective_id=1, has_side_effects=True, vmem_limit_bytes=60 * 2**20
+        ),
+        name="reduce",
+    )(chunks, biases, shared, small)
+
+    def tiles(chunk):
+        return chunk.reshape(-1, D, D).transpose(1, 0, 2).reshape(D, -1)
+
+    chunks = chunks.reshape(local, 2, CHUNK, D).astype(F32)
+    biases = biases.reshape(local, 8, D)
+    grad_up = chunks[:, 0].reshape(local, FF // D, D, D).transpose(0, 2, 1, 3).reshape(local, D, FF)
+    shared = shared.astype(F32)
     return (
         output,
         grad_tokens,
-        small[3, :D],
-        small[4, :D],
-        grad_qkv.astype(F32),
-        small[5, :D],
-        small[5, 2 * D :],
-        grad_table.T,
-        grad_out.astype(F32),
-        small[2, :D],
-        small[0, :D],
-        small[1, :D],
-        grad_router.T,
-        grad_up.astype(F32),
-        grad_up_bias[:, 0],
-        grad_down.astype(F32),
-        grad_down_bias[:, 0],
+        small[3],
+        small[4],
+        tiles(shared[: 3 * D]),
+        small[5],
+        small[7],
+        small[16 : 16 + HEADS, :TABLE].T,
+        shared[3 * D :],
+        small[2],
+        small[0],
+        small[1],
+        small[8:16].T,
+        grad_up,
+        biases[:, : FF // D].reshape(local, FF),
+        chunks[:, 1],
+        biases[:, FF // D],
     )
 
 

time: 548 us -> 427 us (0.78)
  waiting for transfers between devices: 254 us -> 35.8 us
  Pallas kernels: 115 us -> 278 us
  blocking collectives: 120 us -> 42.3 us
  local copies, waits for them, and re-layouts: 17 us -> 51 us
  between operations: 14.2 us -> 0.78 us
  other arithmetic: 17.9 us -> 7 us
    psum x2 -> x0, waiting for transfers between devices: 217 us -> none  [the longest x1 169 us: shards(): grad_up, grad_down = lax.psum((grad_up, grad_down), 'dp')]
    pallas_call x0 -> x1, Pallas kernels: none -> 163 us  [shards(): pl.pallas_call(partial(reduce_kernel, copies, members), in_specs=[vmem] *...]
    psum x2 -> x0, blocking collectives: 77.5 us -> none  [the longest x1 39.1 us: shards(): lax.psum((grad_up_bias, grad_down_bias), 'dp')]
    convert_element_type x6 -> x1, other arithmetic: 15.7 us -> 4.23 us  [shards(): chunks = chunks.reshape(local, 2, CHUNK, D).astype(F32)]
    another operation x0 -> x1, local copies, waits for them, and re-layouts: none -> 7.61 us  [shards(): chunks[:, 0].reshape(local, FF // D, D, D).transpose(0, 2, 1, 3)]
    reshape x0 -> x2, local copies, waits for them, and re-layouts: none -> 7.54 us  [the longest x1 6.37 us: shards(): chunks[:, 0].reshape(local, FF // D, D, D).transpose(0, 2, 1, 3)]
    slice x1 -> x5, local copies, waits for them, and re-layouts: 0.62 us -> 8.08 us  [the longest x1 2.49 us: shards(): chunks[:, 0].reshape(local, FF // D, D, D).transpose(0, 2, 1, 3)]
  transfers between devices with their start and end apart: 3 -> 1, of which waited for: 3 -> 1; matrix products, arithmetic and copies ran while one was open for 2% -> 0% of each run, Pallas kernels for 0% -> 0%
where the time goes in v2:
time: 427 us; the launch traced here: 425 us
  Pallas kernels  278 us (65%)
  local copies, waits for them, and re-layouts  51 us (12%)
  blocking collectives  42.3 us (10%)
  waiting for transfers between devices  35.8 us (8%)
  other arithmetic  7 us (2%)
  matrix products  5.95 us (1%)
  starting transfers between devices  4.34 us (1%)
    pallas_call x1, Pallas kernels, shards(): pl.pallas_call(partial(reduce_kernel, copies, members), in_specs=[vmem] *...  163 us
    pallas_call x1, Pallas kernels, shards(): pl.pallas_call(backward_kernel, grid=(images,), in_specs=[whole((count, D...  53 us
    all_to_all x1, blocking collectives, shards(): lax.all_to_all(back, 'expert', split_axis=0, concat_axis=0, tiled=True)  42.3 us
    all_to_all x1, waiting for transfers between devices, shards(): lax.all_to_all(sending.reshape(members, local, SLOTS, 2 * D), 'expert', s...  35.8 us
    pallas_call x1, Pallas kernels, shards(): pl.pallas_call(expert_kernel, grid=(local, members), in_specs=[per_block,...  28 us
    pallas_call x1, Pallas kernels, shards(): pl.pallas_call(forward_kernel, grid=(images,), in_specs=[whole((count, D)...  23.6 us
    pallas_call x1, Pallas kernels, shards(): pl.pallas_call(dispatch_kernel, grid=(EXPERTS,), in_specs=[whole((images,...  10.7 us
  transfers between devices with their start and end apart: 1, of which 1 were waited for; matrix products, arithmetic and copies ran while one was open for 0% of the time, Pallas kernels for 0%

profile of v2, /device:TPU:0, one launch (start us, length us, event | category | flops | bytes accessed | tf_op | source)
XLA Modules:
  0.0 425.4 jit_solution(3423471626465291618)
XLA Ops:
  0.7 1.3 broadcast_in_dim.31.gain1_ref
  1.9 1.2 broadcast_in_dim.32.bias1_ref
  3.2 1.2 broadcast_in_dim.33.gain2_ref
  4.4 1.2 broadcast_in_dim.34.bias2_ref
  5.7 1.2 broadcast_in_dim.37.out_bias_ref
  6.9 0.7 convert.9
  7.6 0.1 stack.12
  7.7 0.7 add_convert_fusion
  8.5 0.7 pad_maximum_fusion
  9.2 0.6 broadcast_in_dim.36.offset_ref
  9.8 1.5 copy.50.router_ref
  11.3 3.6 convolution_bitcast_fusion
  15.0 0.2 reshape.77
  15.1 0.2 copy.64
  15.4 0.8 reshape.78.relative_ref
  16.2 0.6 pad.8.route_ref
  16.8 23.6 %forward.1 = (bf16[2048,1152]{1,0:T(8,128)(2,1)}, bf16[6144,256]{1,0:T(8,128)(2,1)}, bf16[2048,384]{1,0:T(8,128)(2,1)}, f32[2048,384]{1,0:T(8,128)}, bf16[2048,7...) custom-call(bf16[1568,384]{1,0:T(8,128)(2,1)} %tokens_ref.3, bf16[1568,384]{1,0:T(8,128)(2,1)} %grad_ref.3, ...), custom_call_target="tpu_custom_call" | custom-call | tf_op jit(solution)/shard_map/forward/pallas_call | solution.py:548
  40.4 10.7 %dispatch.1 = bf16[8,256,768]{2,1,0:T(8,128)(2,1)} custom-call(s32[8,8,256]{2,1,0:T(8,128)} %get-tuple-element.41.place_ref, bf16[2048,768]{1,0:T(8,128)(2,1)} %get-tuple-element.42.rows_ref), custom_call_target="tpu_custom_call" | custom-call | tf_op jit(solution)/shard_map/dispatch/pallas_call | solution.py:577
  51.2 4.3 %all-to-all-start = ((bf16[4,2,256,768]{3,2,1,0:T(8,128)(2,1)}), bf16[4,2,256,768]{3,2,1,0:T(8,128)(2,1)S(1)}, u32[]{:S(2)}, u32[]{:S(2)}) async-start(bf16[4,2,256,768]{3,2,1,0:T(8,128)(2,1)} %bitcast.44), calls=%async_computation | async-start | bytes 6291456 | tf_op jit(solution)/shard_map/all_to_all | solution.py:587
  55.5 0.6 broadcast_in_dim.39.down_bias_ref
  56.1 0.6 broadcast_in_dim.38.up_bias_ref
  56.7 35.8 %all-to-all-done.rows_ref = bf16[4,2,256,768]{3,2,1,0:T(8,128)(2,1)S(1)} async-done(((bf16[4,2,256,768]{3,2,1,0:T(8,128)(2,1)}), bf16[4,2,256,768]{3,2,1,0:T(8,128)(2,1)S(1)}, u32[]{:S(2)}, u32[]{:S(2)}) %all-to-all-start) | async-done | bytes 3145760 | tf_op jit(solution)/shard_map/all_to_all | solution.py:587
  92.5 1.7 copy-done.3
  94.2 28.0 %experts.1 = (bf16[4,2,256,768]{3,2,1,0:T(8,128)(2,1)}, bf16[4,1536,384]{2,1,0:T(8,128)(2,1)}, f32[16,384]{1,0:T(8,128)}) custom-call(bf16[4,2,256,768]{3,2,1,0:T(8,128)(2,1)} %copy-done.3, bf16[2,384,1536]{2,1,0:T(8,128)(2,1)} %up_ref.1, f32[2,1,1536]{2,1,0:T(1,128)} %broadcast_in_dim.38.up_bias_ref, bf16[2,1536,384]{2,1,0:T(8,128)(2,1)} %down_ref.1, ...), custom_call_target="tpu_custom_call" | custom-call | tf_op jit(solution)/shard_map/experts/pallas_call | solution.py:595
  122.2 42.3 %all_to_all.10 = bf16[4,2,256,768]{3,2,1,0:T(8,128)(2,1)} all-to-all(bf16[4,2,256,768]{3,2,1,0:T(8,128)(2,1)} %get-tuple-element.43), channel_id=1, replica_groups=mesh['dp'=8,'expert'=4] {'expert'}, dimensions={0} | all-to-all | bytes 6291456 | tf_op jit(solution)/shard_map/all_to_all | solution.py:618
  164.5 53.0 %backward.1 = (bf16[1568,384]{1,0:T(8,128)(2,1)}, f32[1568,384]{1,0:T(8,128)}, bf16[1536,384]{1,0:T(8,128)(2,1)}, f32[64,768]{1,0:T(8,128)}, f32[16,384]{1,0:T(8,128)}) custom-call(bf16[1568,384]{1,0:T(8,128)(2,1)} %tokens_ref.3, bf16[1568,384]{1,0:T(8,128)(2,1)} %grad_ref.3, s32[256,1]{1,0:T(8,128)} %constant.14.clone.source_ref, ...), custom_call_target="tpu_custom_call" | custom-call | tf_op jit(solution)/shard_map/backward/pallas_call | solution.py:621
  217.4 1.1 reshape.81
  218.5 0.9 copy.51
  219.4 1.1 reshape.82
  220.5 2.3 fusion
  222.9 0.6 select_maximum_fusion.small_ref
  223.5 162.9 %reduce.15 = (bf16[4,1536,384]{2,1,0:T(8,128)(2,1)}, f32[16,384]{1,0:T(8,128)}, bf16[1536,384]{1,0:T(8,128)(2,1)}, f32[32,384]{1,0:T(8,128)}) custom-call(bf16[4,1536,384]{2,1,0:T(8,128)(2,1)} %get-tuple-element.46.chunks_ref, f32[16,384]{1,0:T(8,128)} %get-tuple-element.47.biases_ref, bf16[1536,384]{1,0:T(8,128)(2,1)} %get-tuple-element.48.shared_ref, ...), custom_call_target="tpu_custom_call" | custom-call | tf_op jit(solution)/shard_map/reduce/pallas_call | solution.py:658
  386.4 0.9 slice.65
  387.3 1.0 slice_bitcast_fusion.2
  388.3 1.3 slice_bitcast_fusion.3
  389.6 1.6 slice_reduce_fusion
  391.2 1.3 slice_bitcast_fusion.1
  392.5 1.8 slice.61
  394.3 1.3 slice.60
  395.6 2.5 slice.62
  398.1 4.2 convert.11
  402.3 0.6 copy.59
  403.0 0.6 copy.65
  403.5 1.2 copy.52
  404.7 1.9 copy.56
  406.6 7.6 %copy.63 = f32[2,4,384,384]{3,1,2,0:T(4,128)} copy(f32[2,4,384,384]{3,2,1,0:T(8,128)} %bitcast.41) | data formatting | bytes 9437184 | tf_op jit(solution)/shard_map/reshape;squeeze | solution.py:684
  414.2 6.4 %reshape.85 = f32[2,384,1536]{2,1,0:T(8,128)} reshape(f32[2,384,4,384]{3,2,1,0:T(4,128)} %bitcast.42) | data formatting | bytes 9437184 | tf_op jit(solution)/shard_map/reshape | solution.py:684
  420.6 4.8 %slice_bitcast_fusion = f32[2,1536,384]{2,1,0:T(8,128)} fusion(f32[2,2,1536,384]{3,2,1,0:T(8,128)} %convert.11), kind=kLoop, calls=%fused_computation | loop fusion | bytes 9437184 | tf_op jit(solution)/shard_map/squeeze | solution.py:702
  (18 shorter events, 0.2 us)
Async XLA Ops:
  0.7 10.7 %copy-start = (f32[169,12]{0,1:T(8,128)S(1)}, f32[169,12]{0,1:T(8,128)}, u32[]{:S(2)}) copy-start(f32[169,12]{0,1:T(8,128)} %param.28) | copy-start | bytes 24340
  51.2 4.3 %copy-start.7 = (f32[2,384]{1,0:T(2,128)S(1)}, f32[2,384]{1,0:T(2,128)}, u32[]{:S(2)}) copy-start(f32[2,384]{1,0:T(2,128)} %param.37) | copy-start | bytes 9220
  51.2 4.9 %copy-start.6 = (f32[2,1536]{1,0:T(2,128)S(1)}, f32[2,1536]{1,0:T(2,128)}, u32[]{:S(2)}) copy-start(f32[2,1536]{1,0:T(2,128)} %param.35) | copy-start | bytes 36868
  51.2 41.4 %all-to-all-start = ((bf16[4,2,256,768]{3,2,1,0:T(8,128)(2,1)}), bf16[4,2,256,768]{3,2,1,0:T(8,128)(2,1)S(1)}, u32[]{:S(2)}, u32[]{:S(2)}) async-start(bf16[4,2,256,768]{3,2,1,0:T(8,128)(2,1)} %bitcast.44), calls=%async_computation | async-start | bytes 6291456 | tf_op jit(solution)/shard_map/all_to_all | solution.py:587
  92.5 1.7 copy-start.3
  164.4 56.0 %copy-start.4 = (f32[169,4096]{1,0:T(8,128)S(1)}, f32[169,4096]{1,0:T(8,128)}, u32[]{:S(2)}) copy-start(f32[169,4096]{1,0:T(8,128)} %constant.16.clone) | copy-start | bytes 8306692
  217.4 5.4 %copy-start.5 = (f32[16,384]{1,0:T(8,128)S(1)}, f32[16,384]{1,0:T(8,128)}, u32[]{:S(2)}) copy-start(f32[16,384]{1,0:T(8,128)} %get-tuple-element.49) | copy-start | bytes 73732
  386.4 9.2 %copy-start.2 = (bf16[4,1536,384]{2,1,0:T(8,128)(2,1)S(1)}, bf16[4,1536,384]{2,1,0:T(8,128)(2,1)}, u32[]{:S(2)}) copy-start(bf16[4,1536,384]{2,1,0:T(8,128)(2,1)} %get-tuple-element.53) | copy-start | bytes 14155780
  414.2 11.2 %copy-start.1 = (f32[169,12]{0,1:T(8,128)S(1)}, f32[169,12]{0,1:T(8,128)}, u32[]{:S(2)}) copy-start(f32[169,12]{0,1:T(8,128)} %param.28) | copy-start | bytes 24340

commit v3 on v1

v3 whole, which is shorter than its diff:
```python
from functools import partial

import jax
import jax.numpy as jnp
import numpy as np
from jax import lax
from jax.experimental import pallas as pl
from jax.experimental.pallas import tpu as pltpu
from jax.sharding import PartitionSpec as P

D = 384
HEADS = 12
HEAD = 32
FF = 1536
EXPERTS = 8
WINDOW = 7
SIDE = 14
SHIFT = 3
CAP = 245
CELLS = WINDOW * WINDOW
IMAGE = SIDE * SIDE
TABLE = (2 * WINDOW - 1) ** 2

ROWS = 64
SLOTS = 256
FRAME = 4 * ROWS
SPAN = 208
GROUP = 4
GROUPS = HEADS // GROUP
LANES = GROUP * HEAD
WIDE = GROUP * ROWS

EPSILON = 1e-05
MASK_NEG = -100.0
SCALE = HEAD ** (-0.5)
HIGHEST = lax.Precision.HIGHEST
F32 = jnp.float32
BF16 = jnp.bfloat16


def source_cells():
    source = np.full((FRAME, 1), -1000, np.int32)
    for row in range(FRAME):
        window, cell = divmod(row, ROWS)
        if cell < CELLS:
            down = (window // 2) * WINDOW + cell // WINDOW
            across = (window % 2) * WINDOW + cell % WINDOW
            source[row, 0] = ((down + SHIFT) % SIDE) * SIDE + (across + SHIFT) % SIDE
    return source


def window_masks():
    places = np.arange(SIDE)
    bands = (places >= SIDE - WINDOW).astype(np.int32) + (places >= SIDE - SHIFT)
    masks = np.zeros((4, ROWS, ROWS), np.float32)
    for window in range(4):
        rows = bands[(window // 2) * WINDOW : (window // 2 + 1) * WINDOW]
        cols = bands[(window % 2) * WINDOW : (window % 2 + 1) * WINDOW]
        labels = (rows[:, None] * 3 + cols[None, :]).reshape(-1)
        masks[window, :CELLS, :CELLS] = np.where(labels[:, None] != labels[None, :], MASK_NEG, 0.0)
    masks[:, CELLS:, :] = -1e30
    return np.tile(masks, (1, 1, GROUP))


def offset_onehot():
    hot = np.zeros((TABLE, ROWS, ROWS), np.float32)
    for q in range(CELLS):
        for p in range(CELLS):
            entry = (p // WINDOW - q // WINDOW + WINDOW - 1) * (2 * WINDOW - 1)
            entry += p % WINDOW - q % WINDOW + WINDOW - 1
            hot[entry, q, p] = 1.0
    return hot.reshape(TABLE, ROWS * ROWS)


def mm(left, right):
    return jnp.dot(left, right, preferred_element_type=F32)


def mm_nt(left, right):
    return lax.dot_general(left, right, (((1,), (1,)), ((), ())), preferred_element_type=F32)


def mm_tn(left, right):
    return lax.dot_general(left, right, (((0,), (0,)), ((), ())), preferred_element_type=F32)


def permutation(source, offset, width):
    places = lax.broadcasted_iota(jnp.int32, (FRAME, width), 1)
    return jnp.where(source + offset == places, 1.0, 0.0).astype(BF16)


def normalize(values):
    center = values - jnp.mean(values, axis=-1, keepdims=True)
    inverse = lax.rsqrt(jnp.mean(center * center, axis=-1, keepdims=True) + EPSILON)
    return center * inverse, inverse


def normalize_pull(grad, hat, inverse, gain):
    scaled = grad * gain
    first = jnp.mean(scaled, axis=-1, keepdims=True)
    second = jnp.mean(scaled * hat, axis=-1, keepdims=True)
    return (scaled - first - hat * second) * inverse


def spread_heads(block):
    heads = lax.broadcasted_iota(jnp.int32, block.shape, 1) // HEAD
    return jnp.concatenate(
        [jnp.where(heads == h, block, jnp.zeros_like(block)) for h in range(GROUP)], axis=0
    )


def pick_heads(wide):
    heads = lax.broadcasted_iota(jnp.int32, (ROWS, LANES), 1) // HEAD
    picked = wide[:ROWS]
    for h in range(1, GROUP):
        picked = jnp.where(heads == h, wide[h * ROWS : (h + 1) * ROWS], picked)
    return picked


def image_span(image):
    offset = lax.rem(image * (IMAGE % 16), 16)
    return pl.multiple_of(image * IMAGE - offset, 16), offset


def split_three(values):
    high = values.astype(BF16)
    rest = values - high.astype(F32)
    middle = rest.astype(BF16)
    return high, middle, (rest - middle.astype(F32)).astype(BF16)


VECTORS = ("ln1_gain", "ln1_bias", "q_bias", "k_bias", "v_bias", "out_bias", "ln2_gain", "ln2_bias")


def vector(ref, name):
    row = VECTORS.index(name)
    return ref[row : row + 1, :]


def forward_kernel(
    tokens_ref, grad_ref, route_ref, source_ref, vectors_ref, qkv_ref, relative_ref, mask_ref, out_weight_ref, router_ref,
    projected_ref, weights_ref, attended_ref, residual_ref, rows_ref, place_ref, aux_ref,
):
    image = pl.program_id(0)
    start, offset = image_span(image)
    source = source_ref[...]
    order = permutation(source, offset, SPAN)
    inputs = mm(order, tokens_ref[pl.ds(start, SPAN), :])
    upstream = mm(order, grad_ref[pl.ds(start, SPAN), :])

    plain = permutation(source, 0, FRAME)
    route = route_ref[0]
    route_cols = mm_nt(plain, route)
    route_rows = mm_nt(route, plain)
    chosen_col = route_cols[:, 0:1]
    slot_col = route_cols[:, 1:2]
    place_row = jnp.where(
        route_rows[1:2] > 0.5, route_rows[0:1] * SLOTS + route_rows[1:2] - 1.0, -1.0
    )
    place_ref[0] = jnp.broadcast_to(place_row, (8, FRAME)).astype(jnp.int32)
    place_col = jnp.where(slot_col > 0.5, chosen_col * SLOTS + slot_col - 1.0, -1.0)

    hat, _ = normalize(inputs)
    normed = (hat * vector(vectors_ref, "ln1_gain") + vector(vectors_ref, "ln1_bias")).astype(BF16)
    for third, name in enumerate(("q_bias", "k_bias", "v_bias")):
        at = slice(third * D, (third + 1) * D)
        projected_ref[:, at] = (mm(normed, qkv_ref[:, at]) + vector(vectors_ref, name)).astype(BF16)

    for window in range(4):
        rows = slice(window * ROWS, (window + 1) * ROWS)
        for group in range(GROUPS):
            cols = slice(group * LANES, (group + 1) * LANES)
            wide = slice(group * WIDE, (group + 1) * WIDE)
            queries = projected_ref[rows, group * LANES : (group + 1) * LANES]
            keys = projected_ref[rows, D + group * LANES : D + (group + 1) * LANES]
            values = projected_ref[rows, 2 * D + group * LANES : 2 * D + (group + 1) * LANES]
            scores = mm_nt(keys, spread_heads(queries)) * SCALE
            scores = scores + relative_ref[:, wide] + mask_ref[window]
            powers = jnp.exp(scores - jnp.max(scores, axis=0, keepdims=True))
            weights = (powers / jnp.sum(powers, axis=0, keepdims=True)).astype(BF16)
            place = (window * GROUPS + group) * ROWS
            weights_ref[place : place + ROWS, :] = weights
            attended_ref[rows, cols] = pick_heads(mm_tn(weights, values)).astype(BF16)

    residual = inputs + (mm(attended_ref[...], out_weight_ref[...]) + vector(vectors_ref, "out_bias"))
    residual_ref[...] = residual
    hat, _ = normalize(residual)
    normed = (hat * vector(vectors_ref, "ln2_gain") + vector(vectors_ref, "ln2_bias")).astype(BF16)
    logits = sum(mm_nt(normed, part) for part in split_three(router_ref[...]))
    logits = jnp.exp(logits - jnp.max(logits, axis=-1, keepdims=True))
    probs = logits / jnp.sum(logits, axis=-1, keepdims=True)
    experts = lax.broadcasted_iota(jnp.int32, (FRAME, EXPERTS), 1).astype(F32)
    gate = jnp.sum(jnp.where(experts == chosen_col, probs, 0.0), axis=-1, keepdims=True)
    rows_ref[:, :D] = normed
    rows_ref[:, D:] = (gate * upstream).astype(BF16)
    aux_ref[:, 0:EXPERTS] = probs
    aux_ref[:, EXPERTS : EXPERTS + 1] = gate
    aux_ref[:, EXPERTS + 1 : EXPERTS + 2] = place_col
    aux_ref[:, EXPERTS + 2 : EXPERTS + 3] = chosen_col


def backward_kernel(
    copies, members, tokens_ref, grad_ref, source_ref, vectors_ref, qkv_ref, out_weight_ref, router_ref, hot_ref,
    projected_ref, weights_ref, attended_ref, residual_ref, aux_ref, returned_ref, shards_ref,
    output_ref, grad_tokens_ref, chunks_ref, shared_ref, small_ref,
    grad_projected, grad_qkv, grad_out, totals, flat, shared, small, work, landing, shard, small_landing,
    chunks, shared_sum, small_sum,
    chunk_sends, chunk_recvs, scatter_sends, scatter_recvs, gather_sends, gather_recvs, small_sends, small_recvs, writes,
):
    image = pl.program_id(0)
    images = IMAGES
    everyone = [("expert", s) for s in strides(members)] + copy_bits(copies)[0]
    gathers = [
        Gather(shards_ref.at[c], chunks.at[c], CHUNK, chunk_sends.at[c], chunk_recvs.at[c], bits)
        for c, bits in enumerate(chunk_bits(copies, shards_ref.shape[0]))
    ]

    @pl.when(image == 0)
    def _():
        greet([partner(*bit)[1] for bit in everyone])
        for ref in (output_ref, grad_tokens_ref, grad_qkv, grad_out, totals, small):
            ref[...] = jnp.zeros_like(ref)

    def pieces(boundary):
        due = []
        for c, gather in enumerate(gathers):
            step = boundary - c
            if 0 < step < gather.steps:
                due.append(partial(gather.finish, step - 1))
            if 0 <= step < gather.steps:
                due.append(partial(gather.start, step))
        return due

    for boundary in range(images):
        if due := pieces(boundary):

            @pl.when(image == boundary)
            def _(due=due):
                for piece in due:
                    piece()

    start, offset = image_span(image)
    order = permutation(source_ref[...], offset, SPAN)
    inputs = mm(order, tokens_ref[pl.ds(start, SPAN), :])
    upstream = mm(order, grad_ref[pl.ds(start, SPAN), :])
    residual = residual_ref[...]
    aux = aux_ref[...]
    probs = aux[:, 0:EXPERTS]
    gate = aux[:, EXPERTS : EXPERTS + 1]
    place = aux[:, EXPERTS + 1 : EXPERTS + 2].astype(jnp.int32)
    chosen = aux[:, EXPERTS + 2 : EXPERTS + 3]

    slots = lax.broadcasted_iota(jnp.int32, (FRAME, EXPERTS * SLOTS), 1)
    hot = jnp.where(slots == place, 1.0, 0.0).astype(BF16)
    gathered = mm(hot, returned_ref[...])
    combined = gathered[:, :D]
    output = (residual + gate * combined).astype(BF16)
    output_ref[pl.ds(start, SPAN), :] += mm_tn(order, output).astype(BF16)

    hat2, inverse2 = normalize(residual)
    normed2 = (hat2 * vector(vectors_ref, "ln2_gain") + vector(vectors_ref, "ln2_bias")).astype(BF16)
    gate_grad = jnp.sum(upstream * combined, axis=-1, keepdims=True)
    experts = lax.broadcasted_iota(jnp.int32, (FRAME, EXPERTS), 1).astype(F32)
    grad_logits = gate_grad * gate * (jnp.where(experts == chosen, 1.0, 0.0) - probs)
    logits_high, logits_low, _ = split_three(grad_logits)
    small[8:16, :] += mm_tn(logits_high, normed2) + mm_tn(logits_low, normed2)
    router_high, router_low, _ = split_three(router_ref[...])
    grad_normed = (
        gathered[:, D:]
        + mm(logits_high, router_high)
        + mm(logits_low, router_high)
        + mm(logits_high, router_low)
    )
    small[0:1, :] += jnp.sum(grad_normed * hat2, axis=0, keepdims=True)
    small[1:2, :] += jnp.sum(grad_normed, axis=0, keepdims=True)
    grad_residual = upstream + normalize_pull(grad_normed, hat2, inverse2, vector(vectors_ref, "ln2_gain"))
    mixed = grad_residual.astype(BF16)
    grad_out[...] += mm_tn(attended_ref[...], mixed)
    small[2:3, :] += jnp.sum(mixed.astype(F32), axis=0, keepdims=True)
    grad_attended = mm_nt(mixed, out_weight_ref[...]).astype(BF16)

    for window in range(4):
        rows = slice(window * ROWS, (window + 1) * ROWS)
        for group in range(GROUPS):
            cols = slice(group * LANES, (group + 1) * LANES)
            wide = slice(group * WIDE, (group + 1) * WIDE)
            key_cols = slice(D + group * LANES, D + (group + 1) * LANES)
            value_cols = slice(2 * D + group * LANES, 2 * D + (group + 1) * LANES)
            keys = projected_ref[rows, key_cols]
            values = projected_ref[rows, value_cols]
            spread_queries = spread_heads(projected_ref[rows, cols])
            spread_grads = spread_heads(grad_attended[rows, cols])
            at = (window * GROUPS + group) * ROWS
            weights = weights_ref[at : at + ROWS, :]
            exact = weights.astype(F32)
            grad_weights = mm_nt(values, spread_grads)
            grad_scores = exact * (grad_weights - jnp.sum(exact * grad_weights, axis=0, keepdims=True))
            grad_scores = grad_scores.astype(BF16)
            totals[:, wide] += grad_scores.astype(F32)
            grad_projected[rows, value_cols] = mm(weights, spread_grads).astype(BF16)
            grad_projected[rows, key_cols] = (mm(grad_scores, spread_queries) * SCALE).astype(BF16)
            grad_projected[rows, cols] = (pick_heads(mm_tn(grad_scores, keys)) * SCALE).astype(BF16)

    grads = grad_projected[...]
    hat1, inverse1 = normalize(inputs)
    normed1 = (hat1 * vector(vectors_ref, "ln1_gain") + vector(vectors_ref, "ln1_bias")).astype(BF16)
    grad_qkv[...] += mm_tn(normed1, grads)
    column_sums = jnp.sum(grads.astype(F32), axis=0, keepdims=True)
    for third in range(3):
        small[5 + third : 6 + third, :] += column_sums[:, third * D : (third + 1) * D]
    grad_normed = mm_nt(grads, qkv_ref[...])
    small[3:4, :] += jnp.sum(grad_normed * hat1, axis=0, keepdims=True)
    small[4:5, :] += jnp.sum(grad_normed, axis=0, keepdims=True)
    grad_inputs = grad_residual + normalize_pull(grad_normed, hat1, inverse1, vector(vectors_ref, "ln1_gain"))
    high, low, _ = split_three(grad_inputs)
    grad_tokens_ref[pl.ds(start, SPAN), :] += mm_tn(order, high) + mm_tn(order, low)

    @pl.when(image == images - 1)
    def _():
        for third in range(3):
            at = slice(third * D, (third + 1) * D)
            shared[at, :] = grad_qkv[:, at].astype(BF16)
        shared[3 * D :, :] = grad_out[...].astype(BF16)
        flat[...] = jnp.zeros_like(flat)
        for q in range(CELLS):
            for h in range(HEADS):
                flat[h : h + 1, q * ROWS : (q + 1) * ROWS] = totals[q : q + 1, h * ROWS : (h + 1) * ROWS]
        small[16:32, :] = jnp.zeros((16, D), F32)
        table = sum(mm_nt(part, hot_ref[...]) for part in split_three(flat[...]))
        small[16:32, : table.shape[1]] = table

        for gather in gathers:
            for step in range(min(gather.steps, max(0, images - gathers.index(gather))), gather.steps):
                gather.finish(step - 1)
                gather.start(step)
        streams = [Doubling(small, small_sum, small_landing, small_sends, small_recvs, everyone)]
        rest = everyone[1:]
        for part in range(PARTS):
            turn = part * len(rest) // PARTS
            bits = everyone[:1] + rest[turn:] + rest[:turn]
            rows = pl.ds(part * PART, PART)
            scatter = Scatter(
                shared.at[rows], shard.at[part], PART, work.at[part], landing.at[part],
                scatter_sends.at[part], scatter_recvs.at[part], bits,
            )
            gather = Gather(
                shard.at[part], shared_sum.at[rows], PART, gather_sends.at[part], gather_recvs.at[part], bits
            )
            streams.append(Chain(scatter, gather))
        run(streams)
        small_ref[...] = small_sum[...]
        copies_out = [pltpu.make_async_copy(shared_sum, shared_ref, writes.at[len(gathers)])]
        copies_out[0].start()
        for c, gather in enumerate(gathers):
            gather.finish(gather.steps - 1)
            copies_out.append(pltpu.make_async_copy(chunks.at[c], chunks_ref.at[c], writes.at[c]))
            copies_out[-1].start()
        for copy in copies_out:
            copy.wait()


IMAGES = 8
CHUNK = 4 * D
PARTS = 3
PART = CHUNK // PARTS
STEP = 16
MESH = pl.DeviceIdType.MESH


def add_rows(left, left_at, right, right_at, out, out_at, count):
    step = next(s for s in (64, 48, 32, 16) if count % s == 0)

    def body(i, carry):
        here = i * step
        total = left[pl.ds(pl.multiple_of(left_at + here, 16), step), :].astype(F32)
        total = total + right[pl.ds(pl.multiple_of(right_at + here, 16), step), :].astype(F32)
        out[pl.ds(pl.multiple_of(out_at + here, 16), step), :] = total.astype(out.dtype)
        return carry

    lax.fori_loop(0, count // step, body, 0)


def partner(axis, stride):
    index = lax.axis_index(axis)
    bit = lax.rem(lax.div(index, stride), 2)
    return bit, {axis: index + stride - 2 * stride * bit}


def halvings(rows, count):
    sizes = []
    for _ in range(count):
        halved = rows % 32 == 0
        rows = rows // 2 if halved else rows
        sizes.append((rows, halved))
    return sizes


def landing_rows(rows, count):
    return sum(size for size, _ in halvings(rows, count))


def exchange(src, dst, sends, recvs, step, device):
    return pltpu.make_async_remote_copy(
        src_ref=src, dst_ref=dst, send_sem=sends.at[step], recv_sem=recvs.at[step], device_id=device, device_id_type=MESH
    )


def rows_at(ref, start, size):
    return ref.at[pl.ds(pl.multiple_of(start, 16), size)]


class Scatter:
    def __init__(self, source, out, rows, work, landing, sends, recvs, bits):
        self.source, self.out, self.work, self.landing = source, out, work, landing
        self.sends, self.recvs, self.bits = sends, recvs, bits
        self.steps = len(bits)
        self.plan = []
        at = land = 0
        for bit, (size, halved) in zip(bits, halvings(rows, len(bits))):
            b, device = partner(*bit)
            give, keep = (at + (1 - b) * size, at + b * size) if halved else (at, at)
            self.plan.append((give, keep, land, size, device))
            at = 0 if not self.plan[1:] else keep
            land += size

    def copy(self, step):
        give, _, land, size, device = self.plan[step]
        mine = self.work if step else self.source
        return exchange(
            rows_at(mine, give, size), self.landing.at[pl.ds(land, size)], self.sends, self.recvs, step, device
        )

    def start(self, step):
        self.copy(step).start()

    def finish(self, step):
        self.copy(step).wait()
        _, keep, land, size, _ = self.plan[step]
        mine = self.work if step else self.source
        if step == self.steps - 1:
            add_rows(mine, keep, self.landing, land, self.out, 0, size)
        else:
            add_rows(mine, keep, self.landing, land, self.work, keep if step else 0, size)


class Gather:
    def __init__(self, share, out, rows, sends, recvs, bits):
        self.share, self.out, self.sends, self.recvs = share, out, sends, recvs
        self.plan = []
        start = 0
        for bit, (size, halved) in zip(bits, halvings(rows, len(bits))):
            b, device = partner(*bit)
            start = start + b * size if halved else start
            if halved:
                self.plan.insert(0, (start, size, device))
        self.steps = len(self.plan)

    def copy(self, step):
        start, size, device = self.plan[step]
        return exchange(
            rows_at(self.out, start, size), rows_at(self.out, start, size), self.sends, self.recvs, step, device
        )

    def start(self, step):
        if step == 0:
            start, size, _ = self.plan[0]
            self.out[pl.ds(pl.multiple_of(start, 16), size), :] = self.share[...]
        self.copy(step).start()

    def finish(self, step):
        self.copy(step).wait()


class Chain:
    def __init__(self, first, second):
        self.first, self.second, self.steps = first, second, first.steps + second.steps

    def of(self, step):
        return (self.first, step) if step < self.first.steps else (self.second, step - self.first.steps)

    def start(self, step):
        stream, step = self.of(step)
        stream.start(step)

    def finish(self, step):
        stream, step = self.of(step)
        stream.finish(step)


class Doubling:
    def __init__(self, source, out, landing, sends, recvs, bits):
        self.source, self.out, self.landing = source, out, landing
        self.sends, self.recvs, self.bits = sends, recvs, bits
        self.steps = len(bits)

    def copy(self, step):
        device = partner(*self.bits[step])[1]
        return exchange(self.out, self.landing.at[step], self.sends, self.recvs, step, device)

    def start(self, step):
        if step == 0:
            self.out[...] = self.source[...]
        self.copy(step).start()

    def finish(self, step):
        self.copy(step).wait()
        self.out[...] = self.out[...] + self.landing[step]


def run(streams, begun=()):
    at = [0] * len(streams)
    for stream in streams:
        if stream not in begun:
            stream.start(0)
    while any(a < s.steps for a, s in zip(at, streams)):
        for i, stream in enumerate(streams):
            if at[i] < stream.steps:
                stream.finish(at[i])
                at[i] += 1
                if at[i] < stream.steps:
                    stream.start(at[i])


def strides(size):
    return [2**k for k in range(size.bit_length() - 1)]


def copy_bits(copies):
    low = len(strides(copies)) // 2
    all_bits = [("dp", s) for s in strides(copies)]
    return all_bits, all_bits[low : low + 1] + all_bits[:low] + all_bits[low + 1 :]


def chunk_bits(copies, count):
    first, second = copy_bits(copies)
    return [second if c % 4 == 1 else first for c in range(count)]


def greet(devices):
    barrier = pltpu.get_barrier_semaphore()
    for device in devices:
        pl.semaphore_signal(barrier, inc=1, device_id=device, device_id_type=MESH)
    pl.semaphore_wait(barrier, len(devices))


def member_at(members, hop, sign):
    index = lax.axis_index("expert")
    chips = members // 2
    chip = lax.rem(lax.div(index, 2) + sign * (hop // 2) + chips, chips)
    return chip * 2 + lax.rem(lax.rem(index, 2) + hop % 2, 2)


TILE = 512


def experts_kernel(
    copies, members, local, place_ref, rows_ref, up_ref, up_bias_ref, down_ref, down_bias_ref,
    returned_ref, shards_ref, biases_ref,
    outbox, inbox, results, up_sum, down_sum, up_bias_sum, down_bias_sum, chunks, biases, work, landing, bias_landing,
    out_sends, out_recvs, back_sends, back_recvs, chunk_sends, chunk_recvs, bias_sends, bias_recvs,
):
    me = lax.axis_index("expert")
    bits = chunk_bits(copies, 2 * local)
    greet(
        [{"expert": member_at(members, hop, 1)} for hop in range(1, members)]
        + [partner(*bit)[1] for bit in copy_bits(copies)[0]]
    )
    places = jnp.concatenate([place_ref[i, 0:1, :] for i in range(place_ref.shape[0])], axis=1)

    def out_copy(hop, j):
        return pltpu.make_async_remote_copy(
            src_ref=outbox.at[j, hop], dst_ref=inbox.at[j, hop],
            send_sem=out_sends.at[j, hop], recv_sem=out_recvs.at[j, hop],
            device_id={"expert": member_at(members, hop, 1)}, device_id_type=MESH,
        )

    def back_copy(hop, j):
        return pltpu.make_async_remote_copy(
            src_ref=results.at[j, hop], dst_ref=returned_ref.at[me, j],
            send_sem=back_sends.at[j, hop], recv_sem=back_recvs.at[j, hop],
            device_id={"expert": member_at(members, hop, -1)}, device_id_type=MESH,
        )

    def dispatch(hop, j):
        expert = member_at(members, hop, 1) * local + j
        slots = lax.broadcasted_iota(jnp.int32, (SLOTS, places.shape[1]), 0) + expert * SLOTS
        hot = jnp.where(slots == places, 1.0, 0.0).astype(BF16)
        return mm(hot, rows_ref[...]).astype(BF16)

    order = [(hop, j) for j in range(local) for hop in range(members - 1, 1, -1)]
    order += [(hop, j) for j in range(local) for hop in (1, 0)]
    for hop, j in order:
        if hop:
            outbox[j, hop] = dispatch(hop, j)
            out_copy(hop, j).start()
        else:
            inbox[j, 0] = dispatch(0, j)

    up_sum[...] = jnp.zeros_like(up_sum)
    down_sum[...] = jnp.zeros_like(down_sum)
    up_bias_sum[...] = jnp.zeros_like(up_bias_sum)
    down_bias_sum[...] = jnp.zeros_like(down_bias_sum)

    def compute(pair, j):
        hops = (2 * pair, 2 * pair + 1)
        for hop in hops:
            if hop:
                out_copy(hop, j).wait_recv()
        inputs = inbox[j, 2 * pair : 2 * pair + 2, :, :D].reshape(2 * SLOTS, D)
        grads = inbox[j, 2 * pair : 2 * pair + 2, :, D:].reshape(2 * SLOTS, D)
        inputs_t = inputs.T
        grads_t = grads.T
        outs = jnp.zeros((2 * SLOTS, D), F32)
        backs = jnp.zeros((2 * SLOTS, D), F32)
        for tile in range(FF // TILE):
            at = slice(tile * TILE, (tile + 1) * TILE)
            pre = mm(inputs, up_ref[j, :, at]) + up_bias_ref[j : j + 1, at]
            grad_hidden = mm_nt(grads, down_ref[j, at, :])
            share = 0.5 + 0.5 * lax.erf(pre * 0.7071067811865476)
            density = jnp.exp(pre * pre * -0.5) * 0.3989422804014327
            hidden = (pre * share).astype(BF16)
            grad_pre = (grad_hidden * (share + pre * density)).astype(BF16)
            outs += mm(hidden, down_ref[j, at, :])
            backs += mm_nt(grad_pre, up_ref[j, :, at])
            down_sum[j, :, at] += mm(grads_t, hidden)
            up_sum[j, :, at] += mm(inputs_t, grad_pre)
            up_bias_sum[j : j + 1, at] += jnp.sum(grad_pre.astype(F32), axis=0, keepdims=True)
        down_bias_sum[j : j + 1, :] += jnp.sum(grads.astype(F32), axis=0, keepdims=True)
        results[j, 2 * pair : 2 * pair + 2, :, :D] = (
            (outs + down_bias_ref[j : j + 1, :]).astype(BF16).reshape(2, SLOTS, D)
        )
        results[j, 2 * pair : 2 * pair + 2, :, D:] = backs.astype(BF16).reshape(2, SLOTS, D)
        for hop in hops:
            if hop:
                back_copy(hop, j).start()
            else:
                returned_ref[me, j] = results[j, 0]

    def seal(j):
        for tile in range(FF // D):
            at = slice(tile * D, (tile + 1) * D)
            chunks[2 * j, at, :] = up_sum[j, :, at].astype(BF16)
            chunks[2 * j + 1, at, :] = down_sum[j, :, at].T.astype(BF16)
            biases[8 * j + tile : 8 * j + tile + 1, :] = up_bias_sum[j : j + 1, at]
        biases[8 * j + 4 : 8 * j + 5, :] = down_bias_sum[j : j + 1, :]
        biases[8 * j + 5 : 8 * j + 8, :] = jnp.zeros((3, D), F32)

    streams = [
        Scatter(
            chunks.at[c], shards_ref.at[c], CHUNK, work.at[c], landing.at[c], chunk_sends.at[c], chunk_recvs.at[c],
            bits[c],
        )
        for c in range(2 * local)
    ]
    for pair in range(members // 2):
        for j in range(local):
            compute(pair, j)
            if pair == members // 2 - 1:
                seal(j)
                for stream in streams[2 * j : 2 * j + 2]:
                    stream.start(0)
    small = Doubling(biases, biases_ref, bias_landing, bias_sends, bias_recvs, copy_bits(copies)[0])
    run([*streams, small], begun=streams)
    for j in range(local):
        for hop in range(1, members):
            out_copy(hop, j).wait_send()
            back_copy(hop, j).wait()


def finish_kernel(
    up_tile_ref, down_tile_ref, biases_ref, shared_ref, small_ref,
    up_ref, down_ref, up_bias_ref, down_bias_ref, qkv_ref, out_ref, router_ref, table_ref, *vector_refs,
):
    up_ref[0] = up_tile_ref[0].astype(F32)
    down_ref[0] = down_tile_ref[0].astype(F32)

    @pl.when((pl.program_id(0) == 0) & (pl.program_id(1) == 0))
    def _():
        for j in range(up_bias_ref.shape[0]):
            for tile in range(FF // D):
                row = 8 * j + tile
                up_bias_ref[j : j + 1, tile * D : (tile + 1) * D] = biases_ref[row : row + 1, :]
            down_bias_ref[j : j + 1, :] = biases_ref[8 * j + 4 : 8 * j + 5, :]
        for third in range(3):
            at = slice(third * D, (third + 1) * D)
            qkv_ref[:, at] = shared_ref[at, :].astype(F32)
        out_ref[...] = shared_ref[3 * D :, :].astype(F32)
        router_ref[...] = small_ref[8:16, :]
        table_ref[...] = small_ref[16 : 16 + HEADS, :TABLE]
        for ref, row in zip(vector_refs, (3, 4, 5, 7, 2, 0, 1)):
            ref[...] = small_ref[row, :]


def whole(shape):
    return pl.BlockSpec(shape, lambda *_: (0,) * len(shape))


def per_image(rows, columns):
    return pl.BlockSpec((rows, columns), lambda i: (i, 0))


def shards(
    tokens, ln1_gain, ln1_bias, qkv_weight, q_bias, v_bias, bias_table, out_weight, out_bias, ln2_gain, ln2_bias,
    router_weight, up_weight, up_bias, down_weight, down_bias, expert_of, slot_of, grad_output,
):
    members = lax.axis_size("expert")
    local = up_weight.shape[0]
    count = tokens.shape[0]
    images = count // IMAGE
    framed = images * FRAME
    params = pltpu.CompilerParams(dimension_semantics=("arbitrary",), vmem_limit_bytes=60 * 2**20)

    source = jnp.asarray(source_cells())
    masks = jnp.asarray(window_masks())
    hot = jnp.asarray(offset_onehot())
    relative = jnp.dot(bias_table.T, hot, precision=HIGHEST).reshape(HEADS, ROWS, ROWS)
    relative = relative.transpose(1, 0, 2).reshape(ROWS, HEADS * ROWS)
    route = jnp.stack([expert_of, slot_of + 1]).astype(BF16).reshape(2, images, IMAGE).transpose(1, 0, 2)
    route = jnp.pad(route, ((0, 0), (0, 6), (0, FRAME - IMAGE)))
    vectors = jnp.stack(
        [ln1_gain, ln1_bias, q_bias, jnp.zeros_like(q_bias), v_bias, out_bias, ln2_gain, ln2_bias]
    )
    router = router_weight.T
    vmem = pl.BlockSpec(memory_space=pltpu.VMEM)
    dma = pltpu.SemaphoreType.DMA

    projected, weights, attended, residual, rows, place, aux = pl.pallas_call(
        forward_kernel,
        grid=(images,),
        in_specs=[
            whole((count, D)), whole((count, D)), pl.BlockSpec((1, 8, FRAME), lambda i: (i, 0, 0)),
            whole((FRAME, 1)), whole((8, D)), whole((D, 3 * D)), whole((ROWS, HEADS * ROWS)),
            whole((4, ROWS, WIDE)), whole((D, D)), whole((EXPERTS, D)),
        ],
        out_specs=[
            per_image(FRAME, 3 * D), per_image(4 * GROUPS * ROWS, WIDE), per_image(FRAME, D), per_image(FRAME, D),
            per_image(FRAME, 2 * D), pl.BlockSpec((1, 8, FRAME), lambda i: (i, 0, 0)), per_image(FRAME, 128),
        ],
        out_shape=[
            jax.ShapeDtypeStruct((framed, 3 * D), BF16),
            jax.ShapeDtypeStruct((images * 4 * GROUPS * ROWS, WIDE), BF16),
            jax.ShapeDtypeStruct((framed, D), BF16),
            jax.ShapeDtypeStruct((framed, D), F32),
            jax.ShapeDtypeStruct((framed, 2 * D), BF16),
            jax.ShapeDtypeStruct((images, 8, FRAME), jnp.int32),
            jax.ShapeDtypeStruct((framed, 128), F32),
        ],
        compiler_params=params,
        name="forward",
    )(tokens, grad_output, route, source, vectors, qkv_weight, relative, masks, out_weight, router)

    copies = lax.axis_size("dp")
    depth = len(strides(copies))
    total = depth + len(strides(members))
    pieces = 2 * local
    share = halvings(CHUNK, depth)[-1][0]
    returned, shares, biases = pl.pallas_call(
        partial(experts_kernel, copies, members, local),
        in_specs=[vmem] * 6,
        out_specs=[vmem] * 3,
        out_shape=[
            jax.ShapeDtypeStruct((members, local, SLOTS, 2 * D), BF16),
            jax.ShapeDtypeStruct((pieces, share, D), BF16),
            jax.ShapeDtypeStruct((8 * local, D), F32),
        ],
        scratch_shapes=[
            pltpu.VMEM((local, members, SLOTS, 2 * D), BF16),
            pltpu.VMEM((local, members, SLOTS, 2 * D), BF16),
            pltpu.VMEM((local, members, SLOTS, 2 * D), BF16),
            pltpu.VMEM((local, D, FF), F32),
            pltpu.VMEM((local, D, FF), F32),
            pltpu.VMEM((local, FF), F32),
            pltpu.VMEM((local, D), F32),
            pltpu.VMEM((pieces, CHUNK, D), BF16),
            pltpu.VMEM((8 * local, D), F32),
            pltpu.VMEM((pieces, CHUNK // 2, D), BF16),
            pltpu.VMEM((pieces, landing_rows(CHUNK, depth), D), BF16),
            pltpu.VMEM((depth, 8 * local, D), F32),
            dma((local, members)), dma((local, members)), dma((local, members)), dma((local, members)),
            dma((pieces, depth)), dma((pieces, depth)), dma((depth,)), dma((depth,)),
        ],
        compiler_params=pltpu.CompilerParams(
            collective_id=1, has_side_effects=True, vmem_limit_bytes=60 * 2**20
        ),
        name="experts",
    )(place, rows, up_weight, up_bias, down_weight, down_bias)
    returned = returned.reshape(EXPERTS * SLOTS, 2 * D)

    output, grad_tokens, chunks, shared, small = pl.pallas_call(
        partial(backward_kernel, copies, members),
        grid=(images,),
        in_specs=[
            whole((count, D)), whole((count, D)), whole((FRAME, 1)), whole((8, D)), whole((D, 3 * D)), whole((D, D)),
            whole((EXPERTS, D)), whole((TABLE, ROWS * ROWS)),
            per_image(FRAME, 3 * D), per_image(4 * GROUPS * ROWS, WIDE), per_image(FRAME, D), per_image(FRAME, D),
            per_image(FRAME, 128), whole((EXPERTS * SLOTS, 2 * D)), whole((pieces, share, D)),
        ],
        out_specs=[
            whole((count, D)), whole((count, D)), pl.BlockSpec(memory_space=pl.ANY),
            pl.BlockSpec(memory_space=pl.ANY), whole((32, D)),
        ],
        out_shape=[
            jax.ShapeDtypeStruct((count, D), BF16),
            jax.ShapeDtypeStruct((count, D), F32),
            jax.ShapeDtypeStruct((pieces, CHUNK, D), BF16),
            jax.ShapeDtypeStruct((CHUNK, D), BF16),
            jax.ShapeDtypeStruct((32, D), F32),
        ],
        scratch_shapes=[
            pltpu.VMEM((FRAME, 3 * D), BF16), pltpu.VMEM((D, 3 * D), F32), pltpu.VMEM((D, D), F32),
            pltpu.VMEM((ROWS, HEADS * ROWS), F32),
            pltpu.VMEM((16, ROWS * ROWS), F32),
            pltpu.VMEM((CHUNK, D), BF16),
            pltpu.VMEM((32, D), F32),
            pltpu.VMEM((PARTS, PART // 2, D), BF16),
            pltpu.VMEM((PARTS, landing_rows(PART, total), D), BF16),
            pltpu.VMEM((PARTS, halvings(PART, total)[-1][0], D), BF16),
            pltpu.VMEM((total, 32, D), F32),
            pltpu.VMEM((pieces, CHUNK, D), BF16),
            pltpu.VMEM((CHUNK, D), BF16),
            pltpu.VMEM((32, D), F32),
            dma((pieces, depth)), dma((pieces, depth)), dma((PARTS, total)), dma((PARTS, total)),
            dma((PARTS, total)), dma((PARTS, total)), dma((total,)), dma((total,)), dma((pieces + 1,)),
        ],
        compiler_params=pltpu.CompilerParams(
            dimension_semantics=("arbitrary",), collective_id=2, has_side_effects=True, vmem_limit_bytes=60 * 2**20
        ),
        name="backward",
    )(
        tokens, grad_output, source, vectors, qkv_weight, out_weight, router, hot.astype(BF16), projected, weights,
        attended, residual, aux, returned, shares,
    )

    results = pl.pallas_call(
        finish_kernel,
        grid=(local, FF // D),
        in_specs=[
            pl.BlockSpec((1, D, D), lambda j, t: (2 * j, t, 0)), pl.BlockSpec((1, D, D), lambda j, t: (2 * j + 1, t, 0)),
            whole((8 * local, D)), whole((CHUNK, D)), whole((32, D)),
        ],
        out_specs=[
            pl.BlockSpec((1, D, D), lambda j, t: (j, 0, t)), pl.BlockSpec((1, D, D), lambda j, t: (j, t, 0)),
            whole((local, FF)), whole((local, D)), whole((D, 3 * D)), whole((D, D)), whole((EXPERTS, D)),
            whole((HEADS, TABLE)), *[whole((D,))] * 7,
        ],
        out_shape=[
            jax.ShapeDtypeStruct(shape, F32)
            for shape in (
                (local, D, FF), (local, FF, D), (local, FF), (local, D), (D, 3 * D), (D, D), (EXPERTS, D),
                (HEADS, TABLE), *[(D,)] * 7,
            )
        ],
        compiler_params=pltpu.CompilerParams(
            dimension_semantics=("arbitrary", "arbitrary"), vmem_limit_bytes=60 * 2**20
        ),
        name="finish",
    )(chunks, chunks, biases, shared, small)
    grad_up, grad_down, grad_up_bias, grad_down_bias, grad_qkv, grad_out, grad_router, grad_table = results[:8]
    grad_gain1, grad_bias1, grad_q, grad_v, grad_out_bias, grad_gain2, grad_bias2 = results[8:]
    return (
        output, grad_tokens, grad_gain1, grad_bias1, grad_qkv, grad_q, grad_v, grad_table.T, grad_out, grad_out_bias,
        grad_gain2, grad_bias2, grad_router.T, grad_up, grad_up_bias, grad_down, grad_down_bias,
    )


def solution(mesh):
    tokens = P(("dp", "expert"), None)
    expert = P("expert", None, None)
    expert_bias = P("expert", None)
    routes = P(("dp", "expert"))
    return jax.shard_map(
        shards,
        mesh=mesh,
        in_specs=(
            tokens, P(), P(), P(), P(), P(), P(), P(), P(), P(), P(), P(), expert, expert_bias, expert, expert_bias,
            routes, routes, tokens,
        ),
        out_specs=(
            tokens, tokens, P(), P(), P(), P(), P(), P(), P(), P(), P(), P(), P(), expert, expert_bias, expert,
            expert_bias,
        ),
        check_vma=False,
    )
```

time: 548 us -> 296 us (0.54)
  waiting for transfers between devices: 254 us -> 0 us
  Pallas kernels: 115 us -> 274 us
  blocking collectives: 120 us -> 0 us
  other arithmetic: 17.9 us -> 1.43 us
  between operations: 14.2 us -> 1.19 us
  local copies, waits for them, and re-layouts: 17 us -> 11 us
    psum x2 -> x0, waiting for transfers between devices: 217 us -> none  [the longest x1 169 us: shards(): grad_up, grad_down = lax.psum((grad_up, grad_down), 'dp')]
    pallas_call x3, Pallas kernels: 91.1 us -> 250 us  [the longest x1 131 us: shards(): pl.pallas_call(partial(backward_kernel, copies, members), grid=(images,),...]
    psum x2 -> x0, blocking collectives: 77.5 us -> none  [the longest x1 39.1 us: shards(): lax.psum((grad_up_bias, grad_down_bias), 'dp')]
    all_to_all x1 -> x0, blocking collectives: 42.3 us -> none  [shards(): lax.all_to_all(back, 'expert', split_axis=0, concat_axis=0, tiled=True)]
    all_to_all x1 -> x0, waiting for transfers between devices: 35.8 us -> none  [shards(): lax.all_to_all(sending.reshape(members, local, SLOTS, 2 * D), 'expert', s...]
    convert_element_type x6 -> x0, other arithmetic: 15.7 us -> none  [the longest x1 4.65 us: shards(): grad_up.astype(F32)]
    broadcast_in_dim x9 -> x0, local copies, waits for them, and re-layouts: 8.02 us -> none  [the longest x5 6.23 us: shards(): row = lambda v: v[None]]
  transfers between devices with their start and end apart: 3 -> 0, of which waited for: 3 -> 0; matrix products, arithmetic and copies ran while one was open for 2% -> 0% of each run, Pallas kernels for 0% -> 0%
where the time goes in v3:
time: 296 us; the launch traced here: 292 us
  Pallas kernels  274 us (93%)
  local copies, waits for them, and re-layouts  11 us (4%)
  matrix products  3.62 us (1%)
    pallas_call x1, Pallas kernels, shards(): pl.pallas_call(partial(backward_kernel, copies, members), grid=(images,),...  131 us
    pallas_call x1, Pallas kernels, shards(): pl.pallas_call(partial(experts_kernel, copies, members, local), in_specs=...  110 us
    pallas_call x1, Pallas kernels, shards(): pl.pallas_call(forward_kernel, grid=(images,), in_specs=[whole((count, D)...  24.3 us
    pallas_call x1, Pallas kernels, shards(): pl.pallas_call(finish_kernel, grid=(local, FF // D), in_specs=[pl.BlockSp...  9.23 us

profile of v3, /device:TPU:0, one launch (start us, length us, event | category | flops | bytes accessed | tf_op | source)
XLA Modules:
  0.0 291.5 jit_solution(5369495397606561668)
XLA Ops:
  0.7 0.0 copy-start
  0.7 0.7 stack.33
  1.4 0.7 stack.34
  2.0 0.7 stack.35
  2.7 0.7 stack.36
  3.4 0.7 stack.37
  4.1 0.7 stack.38
  4.8 0.7 stack.39
  5.5 0.6 stack.40.vectors_ref
  6.1 0.7 convert.8
  6.8 0.1 stack.44
  6.9 0.7 add_convert_fusion
  7.6 0.1 stack.45
  7.7 0.6 pad.4.route_ref
  8.3 0.0 copy-done
  8.3 3.6 %convolution_bitcast_fusion = f32[12,4096]{1,0:T(8,128)S(1)} fusion(f32[169,4096]{1,0:T(8,128)} %constant.15.clone, f32[169,12]{0,1:T(8,128)S(1)} %copy-done), kind=kOutput, calls=%fused_computation | convolution fusion | flops 99680256 | bytes 2973616 | tf_op jit(solution)/shard_map/dot_general | solution.py:716
  12.0 0.2 reshape.50
  12.1 0.2 copy.44
  12.4 0.8 reshape.51.relative_ref
  13.2 24.3 %forward.1 = (bf16[2048,1152]{1,0:T(8,128)(2,1)}, bf16[6144,256]{1,0:T(8,128)(2,1)}, bf16[2048,384]{1,0:T(8,128)(2,1)}, f32[2048,384]{1,0:T(8,128)}, bf16[2048,7...) custom-call(bf16[1568,384]{1,0:T(8,128)(2,1)} %tokens_ref.3, bf16[1568,384]{1,0:T(8,128)(2,1)} %grad_ref.3, ...), custom_call_target="tpu_custom_call" | custom-call | tf_op jit(solution)/shard_map/forward/pallas_call | solution.py:727
  37.5 110.2 %experts.1 = (bf16[4,2,256,768]{3,2,1,0:T(8,128)(2,1)}, bf16[4,192,384]{2,1,0:T(8,128)(2,1)}, f32[16,384]{1,0:T(8,128)}) custom-call(s32[8,8,256]{2,1,0:T(8,128)} %get-tuple-element.52.place_ref, bf16[2048,768]{1,0:T(8,128)(2,1)} %get-tuple-element.53.rows_ref, bf16[2,384,1536]{2,1,0:T(8,128)(2,1)} %up_ref.1, f32[2,1536]{1,0:T(2,128)} %up_bias_ref.1, ...), custom_call_target="tpu_custom_call" | custom-call | tf_op jit(solution)/shard_map/experts/pallas_call | solution.py:757
  147.6 130.6 %backward.1 = (bf16[1568,384]{1,0:T(8,128)(2,1)}, f32[1568,384]{1,0:T(8,128)}, bf16[4,1536,384]{2,1,0:T(8,128)(2,1)}, bf16[1536,384]{1,0:T(8,128)(2,1)}, f32[32,384]{1,0:T(8,128)}) custom-call(bf16[1568,384]{1,0:T(8,128)(2,1)} %tokens_ref.3, bf16[1568,384]{1,0:T(8,128)(2,1)} %grad_ref.3, s32[256,1]{1,0:T(8,128)} %constant.13.clone.source_ref, ...), custom_call_target="tpu_custom_call" | custom-call | tf_op jit(solution)/shard_map/backward/pallas_call | solution.py:789
  278.3 0.0 copy-start.2
  278.3 9.2 %finish.1 = (f32[2,384,1536]{2,1,0:T(8,128)}, f32[2,1536,384]{2,1,0:T(8,128)}, f32[2,1536]{1,0:T(2,128)}, f32[2,384]{1,0:T(2,128)}, f32[384,1152]{1,0:T(8,128)},...) custom-call(bf16[4,1536,384]{2,1,0:T(8,128)(2,1)} %get-tuple-element, ...), custom_call_target="tpu_custom_call" | custom-call | tf_op jit(solution)/shard_map/finish/pallas_call | solution.py:834
  287.5 0.0 copy-start.1
  287.6 0.0 copy-done.2
  287.6 1.0 copy.47
  288.6 1.1 copy-done.1
  289.7 1.4 copy.48
  (2 shorter events, 0.0 us)
Async XLA Ops:
  0.7 7.7 %copy-start = (f32[169,12]{0,1:T(8,128)S(1)}, f32[169,12]{0,1:T(8,128)}, u32[]{:S(2)}) copy-start(f32[169,12]{0,1:T(8,128)} %param.28) | copy-start | bytes 24340
  278.3 9.3 %copy-start.2 = (bf16[1568,384]{1,0:T(8,128)(2,1)S(1)}, bf16[1568,384]{1,0:T(8,128)(2,1)}, u32[]{:S(2)}) copy-start(bf16[1568,384]{1,0:T(8,128)(2,1)} %get-tuple-element.94) | copy-start | bytes 3612676
  287.5 2.1 copy-start.1
